TPU v7x, 256 devices: a whole 4x4x8 slice. The times are simulated.
256 devices in a mesh: ta: 128 (over y, x_hi, z, core), lv: 2 (over x_lo).
Axes of the slice: x: 4 (x_hi: 2, x_lo: 2; x = x_hi * 2 + x_lo), y: 4, z: 8, core: 2. Of those that a mesh axis runs over, the one named last changes fastest.
Arguments:
- wind_field: float32 [2, 4096, 31, 360], P('lv', 'ta'), may hold values from -6 to 6
- band_mask: int32 [2, 128, 4096], P(None, 'ta'), may hold values from 0 to 1, as said below
- sym_flag: int32 [16], replicated, may hold values from 0 to 1
Outputs:
- kelvin_wind: float32 [2, 4096, 31, 360], P('lv', 'ta')
- mjo_wind: float32 [2, 4096, 31, 360], P('lv', 'ta')
- shear_mjo: float32 [4096, 31, 360], P(('ta', 'lv'))
Inputs may be any that keep to these rules, and one draw needn't show every extreme that they name: `band_mask`: for each band and wavenumber, the entries equal to 1 form one run of consecutive frequency indices holding at least one entry and not wrapping past index 4095.
All inputs are finite; a program needn't handle non-finite values.
Results may differ from a plain program's by a relative error of at most 0.0001.
Values sent between devices are 32-bit elements; how exact they have to be, the bound alone decides.
No kernel may reach another device: no remote copies, remote signals or barrier semaphores. Data moves between devices by JAX's collectives and lax.ppermute only.
A program may use at most 64 MiB of HBM per device.

v0:
```python
import functools

import jax
import jax.numpy as jnp
import ml_dtypes
import numpy as np
from jax import lax
from jax.experimental import pallas as pl
from jax.experimental.pallas import tpu as pltpu
from jax.sharding import PartitionSpec as P

NLON = 360
NLAT = 31
KM = 128
NT = 4096
NPAIR = 16
BLOCK = 32
HALF = 16
CENTRE = NPAIR - 1
F32 = jnp.float32
BF16 = jnp.bfloat16


def halves(table):
    table = np.asarray(table, np.float32)
    high = table.astype(ml_dtypes.bfloat16)
    low = (table - high.astype(np.float32)).astype(ml_dtypes.bfloat16)
    return np.stack([high, low])


def turn(rows, cols, length):
    angle = 2.0 * np.pi / length * (np.outer(rows, cols) % length)
    return np.cos(angle), np.sin(angle)


def zonal_forward_table():
    cosine, sine = turn(np.arange(KM), np.arange(NLON), NLON)
    return halves(np.concatenate([cosine, -sine]) / NLON)


def zonal_inverse_table():
    cosine, sine = turn(np.arange(KM), np.arange(NLON), NLON)
    doubled = np.where(np.arange(KM) == 0, 1.0, 2.0)[:, None]
    return halves(np.concatenate([cosine * doubled, -sine * doubled]))


def outer_tables():
    cosine, sine = turn(np.arange(128), np.arange(128), 128)
    forward = np.block([[cosine, sine], [-sine, cosine]])
    inverse = np.block([[cosine, -sine], [sine, cosine]]) / NT
    return halves(forward), halves(inverse)


def inner_tables():
    cosine, sine = turn(np.arange(BLOCK), np.arange(BLOCK), BLOCK)
    eye = np.eye(4)
    cos4, sin4 = np.kron(eye, cosine), np.kron(eye, sine)
    forward = np.block([[cos4, -sin4], [sin4, cos4]])
    order = np.arange(128).reshape(4, 2, HALF).transpose(1, 0, 2).reshape(-1)
    cos4, sin4 = cos4[:, order], sin4[:, order]
    inverse = np.block([[cos4, sin4], [-sin4, cos4]])
    return halves(forward), halves(inverse)


def twist_tables():
    time = np.tile(np.arange(BLOCK), 4)
    order = np.arange(128).reshape(4, 2, HALF).transpose(1, 0, 2).reshape(-1)
    cosine, sine = turn(np.arange(128), time, NT)
    forward = np.stack([cosine, -sine])
    inverse = np.stack([cosine[:, order], sine[:, order]])
    return np.concatenate([forward, inverse]).astype(np.float32)


def split(value):
    high = value.astype(BF16)
    return high, (value - high.astype(F32)).astype(BF16)


def product(left, right, contract):
    dims = (contract, ((), ()))

    def dot(a, b):
        return lax.dot_general(a, b, dims, preferred_element_type=F32)

    return dot(left[0], right[0]) + (dot(left[0], right[1]) + dot(left[1], right[0]))


ROWS_COLS = ((1,), (0,))
ROWS_ROWS = ((1,), (1,))
COLS_COLS = ((0,), (0,))


def zonal_kernel(sym_ref, wind_ref, table_ref, out_ref):
    parts = []
    for j in range(NPAIR):
        sign = 1.0 - 2.0 * sym_ref[j].astype(F32)
        parts.append(0.5 * (wind_ref[CENTRE + j] + sign * wind_ref[CENTRE - j]))
    component = split(jnp.concatenate(parts, axis=0))
    coef = product((table_ref[0], table_ref[1]), component, ROWS_ROWS)
    for c in range(2):
        for jq in range(4):
            tile = coef[c * 128 : (c + 1) * 128, jq * 128 : (jq + 1) * 128]
            out_ref[pl.ds(c * 4 + jq, 128, stride=8), :] = tile


def time_kernel(
    series_ref, mask_ref, spread_ref, outer_f, inner_f, inner_i, outer_i, twist_ref, out_ref
):
    def rows(ref):
        return ref[0], ref[1]

    def wide(c):
        return jnp.concatenate(
            [series_ref[pl.ds(c * 4 + jq, 128, stride=8), :] for jq in range(4)], axis=1
        )

    operand = split(jnp.concatenate([wide(0), wide(1)], axis=0))
    partial = product(rows(outer_f), operand, ROWS_COLS)
    twisted = []
    for jq in range(4):
        lanes = slice(jq * 128, (jq + 1) * 128)
        real, imag = partial[:128, lanes], partial[128:, lanes]
        twisted.append(
            jnp.concatenate(
                [
                    real * twist_ref[0] - imag * twist_ref[1],
                    real * twist_ref[1] + imag * twist_ref[0],
                ],
                axis=1,
            )
        )
    spectrum = product(split(jnp.concatenate(twisted, axis=0)), rows(inner_f), ROWS_COLS)
    low_lanes = lax.broadcasted_iota(jnp.int32, (128, 128), 1) < 64
    for b in range(2):
        keep = lax.dot_general(
            mask_ref[b].astype(F32).astype(BF16),
            spread_ref[...],
            (COLS_COLS, ((), ())),
            preferred_element_type=F32,
        )
        keep = jnp.concatenate([jnp.concatenate([keep, keep], axis=1)] * 4, axis=0)
        unwound = product(split(spectrum * keep), rows(inner_i), ROWS_COLS)
        real_tiles, imag_tiles = [], []
        for jq in range(4):
            real = unwound[jq * 128 : (jq + 1) * 128, :128]
            imag = unwound[jq * 128 : (jq + 1) * 128, 128:]
            real_tiles.append(real * twist_ref[2] - imag * twist_ref[3])
            imag_tiles.append(real * twist_ref[3] + imag * twist_ref[2])

        def regroup(tiles):
            first = [
                jnp.where(low_lanes, tiles[2 * jh], pltpu.roll(tiles[2 * jh + 1], 64, 1))
                for jh in range(2)
            ]
            second = [
                jnp.where(low_lanes, pltpu.roll(tiles[2 * jh], 64, 1), tiles[2 * jh + 1])
                for jh in range(2)
            ]
            return jnp.concatenate(first + second, axis=1)

        stacked = jnp.concatenate([regroup(real_tiles), regroup(imag_tiles)], axis=0)
        restored = product(rows(outer_i), split(stacked), ROWS_COLS)
        for th in range(2):
            for c in range(2):
                for jh in range(2):
                    row = ((b * 2 + th) * 2 + c) * 2 + jh
                    lanes = slice((th * 2 + jh) * 128, (th * 2 + jh + 1) * 128)
                    out_ref[pl.ds(row, 128, stride=16), :] = restored[c * 128 : (c + 1) * 128, lanes]


def write_rows(out_ref, waves, sym_ref):
    for j in range(NPAIR):
        block = waves[j * HALF : (j + 1) * HALF, :]
        out_ref[CENTRE + j] = block
        if j:
            sign = 1.0 - 2.0 * sym_ref[j].astype(F32)
            out_ref[CENTRE - j] = sign * block


def waves_kernel(sym_ref, coef_ref, table_ref, kelvin_ref, mjo_ref):
    th = pl.program_id(0)
    table = (table_ref[0], table_ref[1])
    for b, out_ref in ((0, kelvin_ref), (1, mjo_ref)):
        row = (b * 2 + th) * 4
        coef = jnp.concatenate(
            [
                jnp.concatenate(
                    [coef_ref[pl.ds(row + c * 2 + jh, 128, stride=16), :] for jh in range(2)],
                    axis=1,
                )
                for c in range(2)
            ],
            axis=0,
        )
        write_rows(out_ref, product(split(coef), table, COLS_COLS), sym_ref)


def pick_kernel(level_ref, coef_ref, own_ref, other_ref):
    level = level_ref[0]
    for out_ref, th in ((own_ref, level), (other_ref, 1 - level)):
        for r in range(4):
            out_ref[pl.ds(r * 128, 128), :] = coef_ref[pl.ds(8 + th * 4 + r, 128, stride=16), :]


def shear_kernel(level_ref, sym_ref, own_ref, partner_ref, table_ref, out_ref):
    sign = 2.0 * level_ref[0].astype(F32) - 1.0
    apart = sign * (own_ref[...] - partner_ref[...])
    coef = jnp.concatenate(
        [
            jnp.concatenate([apart[c * 256 : c * 256 + 128], apart[c * 256 + 128 : c * 256 + 256]], axis=1)
            for c in range(2)
        ],
        axis=0,
    )
    waves = product(split(coef), (table_ref[0], table_ref[1]), COLS_COLS)
    write_rows(out_ref, waves, sym_ref)


SMEM = pl.BlockSpec(memory_space=pltpu.SMEM)
VMEM = pl.BlockSpec(memory_space=pltpu.VMEM)


def call(kernel, in_specs, out_shapes, macs, moved, **kwargs):
    return pl.pallas_call(
        kernel,
        in_specs=in_specs,
        out_shape=out_shapes,
        cost_estimate=pl.CostEstimate(flops=2 * macs, bytes_accessed=moved, transcendentals=0),
        compiler_params=pltpu.CompilerParams(vmem_limit_bytes=32 << 20),
        **kwargs,
    )


def shape(*sizes):
    return jax.ShapeDtypeStruct(sizes, F32)


def body(wind_field, band_mask, sym_flag):
    level = lax.axis_index("lv").astype(jnp.int32).reshape(1)
    record = jnp.transpose(wind_field[0], (1, 0, 2))
    outer_f, outer_i = outer_tables()
    inner_f, inner_i = inner_tables()
    spread = np.tile(np.eye(BLOCK), (1, 4)).astype(ml_dtypes.bfloat16)
    inverse_table = zonal_inverse_table()

    coef = call(zonal_kernel, [SMEM, VMEM, VMEM], shape(1024, 128), 3 * 512 * 360 * 256, 3 << 20, out_specs=VMEM)(
        sym_flag, record, zonal_forward_table()
    )
    series = lax.all_to_all(coef, "ta", split_axis=0, concat_axis=0, tiled=True)
    filtered = call(
        time_kernel, [VMEM] * 8, shape(2048, 128), 3 * 4 * 512 * 256 * 256, 4 << 20, out_specs=VMEM
    )(
        series,
        band_mask.reshape(2, BLOCK, 128),
        spread,
        outer_f,
        inner_f,
        inner_i,
        outer_i,
        twist_tables(),
    )
    returned = lax.all_to_all(filtered, "ta", split_axis=0, concat_axis=0, tiled=True)
    own, other = call(
        pick_kernel, [SMEM, VMEM], (shape(512, 128), shape(512, 128)), 1 << 10, 1 << 20, out_specs=(VMEM, VMEM)
    )(level, returned)
    partner = lax.ppermute(other, "lv", [(0, 1), (1, 0)])
    block = pl.BlockSpec((NLAT, HALF, NLON), lambda i: (0, i, 0))
    kelvin, mjo = call(
        waves_kernel,
        [SMEM, VMEM, VMEM],
        (shape(NLAT, BLOCK, NLON), shape(NLAT, BLOCK, NLON)),
        3 * 1024 * 360 * 256,
        5 << 20,
        grid=(2,),
        out_specs=(block, block),
    )(sym_flag, returned, inverse_table)
    shear = call(
        shear_kernel, [SMEM, SMEM, VMEM, VMEM, VMEM], shape(NLAT, HALF, NLON), 3 * 256 * 360 * 256, 2 << 20, out_specs=VMEM
    )(level, sym_flag, own, partner, inverse_table)
    return (
        jnp.transpose(kelvin, (1, 0, 2))[None],
        jnp.transpose(mjo, (1, 0, 2))[None],
        jnp.transpose(shear, (1, 0, 2)),
    )


def solution(mesh):
    placed = (P("lv", "ta", None, None), P(None, "ta", None), P())
    return jax.shard_map(
        body,
        mesh=mesh,
        in_specs=placed,
        out_specs=(
            P("lv", "ta", None, None),
            P("lv", "ta", None, None),
            P(("ta", "lv"), None, None),
        ),
        check_vma=False,
    )
```

profile of v0, /device:TPU:1, one launch (start us, length us, event | category | flops | bytes accessed | tf_op | source)
XLA Modules:
  0.0 94.1 jit_solution(15283221466799592897)
XLA Ops:
  0.6 0.0 copy-start
  0.6 1.4 %copy-done = f32[1,32,31,360]{3,1,2,0:T(8,128)S(1)} copy-done((f32[1,32,31,360]{3,1,2,0:T(8,128)S(1)}, f32[1,32,31,360]{3,1,2,0:T(8,128)}, u32[]{:S(2)}) %copy-start) | copy-done | bytes 1428504
  2.0 0.0 copy-start.2
  2.0 1.0 %copy-done.2 = bf16[2,256,360]{2,1,0:T(8,128)(2,1)S(1)} copy-done((bf16[2,256,360]{2,1,0:T(8,128)(2,1)S(1)}, bf16[2,256,360]{2,1,0:T(8,128)(2,1)}, u32[]{:S(2)}) %copy-start.2) | copy-done | bytes 368664
  3.0 0.0 copy-start.3
  3.0 0.7 copy-done.3
  3.7 0.0 copy-start.5
  3.7 0.0 copy-start.6
  3.7 0.0 copy-start.7
  3.7 0.0 copy-start.8
  3.7 0.0 copy-start.9
  3.7 0.0 copy-start.10
  3.7 0.0 copy-start.11
  3.7 1.2 %shard_map.130 = f32[1024,128]{1,0:T(8,128)S(1)} custom-call(s32[16]{0:T(128)S(1)} %copy-done.3, f32[31,32,360]{2,1,0:T(8,128)S(1)} %bitcast.19, bf16[2,256,360]{2,1,0:T(8,128)(2,1)S(1)} %copy-done.2), custom_call_target="tpu_custom_call" | custom-call | flops 283115520 | bytes 3145728 | tf_op jit(solution)/shard_map/pallas_call | solution.py:246
  4.9 37.7 %all_to_all.22 = f32[128,8,128]{2,1,0:T(8,128)S(1)} all-to-all(f32[128,8,128]{2,1,0:T(8,128)S(1)} %bitcast.18), channel_id=1, replica_groups=mesh['ta'=128,'lv'=2] {'ta'}, dimensions={0} | all-to-all | bytes 1048576 | tf_op jit(solution)/shard_map/all_to_all | solution.py:249
  42.6 0.0 copy-done.5
  42.6 0.0 copy-done.6
  42.6 0.0 copy-done.7
  42.6 0.0 copy-done.8
  42.6 0.0 copy-done.9
  42.6 0.0 copy-done.10
  42.6 0.0 copy-done.11
  42.6 4.1 %shard_map.131 = f32[2048,128]{1,0:T(8,128)} custom-call(f32[1024,128]{1,0:T(8,128)S(1)} %bitcast.20, s32[2,32,128]{2,1,0:T(8,128)S(1)} %bitcast.21, bf16[32,128]{1,0:T(8,128)(2,1)S(1)} %copy-done.11, bf16[2,256,256]{2,1,0:T(8,128)(2,1)S(1)} %copy-done.6, bf16[2,256,256]{2,1,0:T(8,128)(2,1)S(1)} %copy-done.7, bf16[2,256,256]{2,1,0:T(8,128)(2,1)S(1)} %copy-done.8, ...), custom_call_target="tpu_custom_call" | custom-call | flops 805306368 | bytes 4194304 | tf_op jit(solution)/shard_map/pallas_call | solution.py:250
  46.7 0.0 copy-start.1
  46.7 0.0 copy-start.4
  46.7 5.5 %all-to-all-start.1 = ((f32[128,16,128]{2,1,0:T(8,128)}), f32[128,16,128]{2,1,0:T(8,128)S(1)}, u32[]{:S(2)}, u32[]{:S(2)}) async-start(f32[128,16,128]{2,1,0:T(8,128)} %bitcast.5), calls=%async_computation.1 | async-start | bytes 2097152 | tf_op jit(solution)/shard_map/all_to_all | solution.py:262
  52.2 31.7 %all-to-all-done.1 = f32[128,16,128]{2,1,0:T(8,128)S(1)} async-done(((f32[128,16,128]{2,1,0:T(8,128)}), f32[128,16,128]{2,1,0:T(8,128)S(1)}, u32[]{:S(2)}, u32[]{:S(2)}) %all-to-all-start.1) | async-done | bytes 1048608 | tf_op jit(solution)/shard_map/all_to_all | solution.py:262
  83.9 0.2 shard_map.133
  84.0 0.4 collective-permute-start
  84.4 0.0 copy-done.1
  84.4 0.0 copy-done.4
  84.4 3.1 %shard_map.132 = (f32[31,32,360]{2,1,0:T(8,128)}, f32[31,32,360]{2,1,0:T(8,128)}) custom-call(s32[16]{0:T(128)S(1)} %copy-done.4, f32[2048,128]{1,0:T(8,128)S(1)} %bitcast.17, bf16[2,256,360]{2,1,0:T(8,128)(2,1)S(1)} %copy-done.1), custom_call_target="tpu_custom_call" | custom-call | flops 566231040 | bytes 5242880 | tf_op jit(solution)/shard_map/pallas_call | solution.py:268
  87.5 4.8 %collective-permute-done.partner_ref = f32[512,128]{1,0:T(8,128)S(1)} collective-permute-done((f32[512,128]{1,0:T(8,128)S(1)}, f32[512,128]{1,0:T(8,128)S(1)}, u32[]{:S(2)}, u32[]{:S(2)}) %collective-permute-start) | collective-permute-done | bytes 262176 | tf_op jit(solution)/shard_map/ppermute | solution.py:266
  92.3 1.8 %shard_map.134 = f32[31,16,360]{2,1,0:T(8,128)} custom-call(s32[1]{0:T(128)} %bitcast.11.level_ref, s32[16]{0:T(128)S(1)} %copy-done.4, f32[512,128]{1,0:T(8,128)S(1)} %get-tuple-element.9.own_ref, f32[512,128]{1,0:T(8,128)S(1)} %collective-permute-done.partner_ref, bf16[2,256,360]{2,1,0:T(8,128)(2,1)S(1)} %copy-done.1), custom_call_target="tpu_custom_call" | custom-call | flops 141557760 | bytes 2097152 | tf_op jit(solution)/shard_map/pallas_call | solution.py:277
Async XLA Ops:
  0.6 1.4 %copy-start = (f32[1,32,31,360]{3,1,2,0:T(8,128)S(1)}, f32[1,32,31,360]{3,1,2,0:T(8,128)}, u32[]{:S(2)}) copy-start(f32[1,32,31,360]{3,1,2,0:T(8,128)} %param.11) | copy-start | bytes 4285444
  2.0 1.0 %copy-start.2 = (bf16[2,256,360]{2,1,0:T(8,128)(2,1)S(1)}, bf16[2,256,360]{2,1,0:T(8,128)(2,1)}, u32[]{:S(2)}) copy-start(bf16[2,256,360]{2,1,0:T(8,128)(2,1)} %constant.20.clone.table_ref) | copy-start | bytes 1105924
  3.0 0.7 copy-start.3
  3.7 38.9 %copy-start.5 = (s32[2,1,4096]{2,1,0:T(1,128)S(1)}, s32[2,1,4096]{2,1,0:T(1,128)}, u32[]{:S(2)}) copy-start(s32[2,1,4096]{2,1,0:T(1,128)} %param.12) | copy-start | bytes 98308
  3.7 38.9 %copy-start.6 = (bf16[2,256,256]{2,1,0:T(8,128)(2,1)S(1)}, bf16[2,256,256]{2,1,0:T(8,128)(2,1)}, u32[]{:S(2)}) copy-start(bf16[2,256,256]{2,1,0:T(8,128)(2,1)} %constant.22.clone.outer_f) | copy-start | bytes 786436
  3.7 38.9 %copy-start.7 = (bf16[2,256,256]{2,1,0:T(8,128)(2,1)S(1)}, bf16[2,256,256]{2,1,0:T(8,128)(2,1)}, u32[]{:S(2)}) copy-start(bf16[2,256,256]{2,1,0:T(8,128)(2,1)} %constant.23.clone.inner_f) | copy-start | bytes 786436
  3.7 38.9 %copy-start.8 = (bf16[2,256,256]{2,1,0:T(8,128)(2,1)S(1)}, bf16[2,256,256]{2,1,0:T(8,128)(2,1)}, u32[]{:S(2)}) copy-start(bf16[2,256,256]{2,1,0:T(8,128)(2,1)} %constant.24.clone.inner_i) | copy-start | bytes 786436
  3.7 38.9 %copy-start.9 = (bf16[2,256,256]{2,1,0:T(8,128)(2,1)S(1)}, bf16[2,256,256]{2,1,0:T(8,128)(2,1)}, u32[]{:S(2)}) copy-start(bf16[2,256,256]{2,1,0:T(8,128)(2,1)} %constant.25.clone.outer_i) | copy-start | bytes 786436
  3.7 38.9 %copy-start.10 = (f32[4,128,128]{2,1,0:T(8,128)S(1)}, f32[4,128,128]{2,1,0:T(8,128)}, u32[]{:S(2)}) copy-start(f32[4,128,128]{2,1,0:T(8,128)} %constant.26.clone.twist_ref) | copy-start | bytes 786436
  3.7 38.9 %copy-start.11 = (bf16[32,128]{1,0:T(8,128)(2,1)S(1)}, bf16[32,128]{1,0:T(8,128)(2,1)}, u32[]{:S(2)}) copy-start(bf16[32,128]{1,0:T(8,128)(2,1)} %constant.21.clone.spread_ref) | copy-start | bytes 24580
  46.7 37.7 %copy-start.1 = (bf16[2,256,360]{2,1,0:T(8,128)(2,1)S(1)}, bf16[2,256,360]{2,1,0:T(8,128)(2,1)}, u32[]{:S(2)}) copy-start(bf16[2,256,360]{2,1,0:T(8,128)(2,1)} %constant.27.clone.table_ref) | copy-start | bytes 1105924
  46.7 37.7 %copy-start.4 = (s32[16]{0:T(128)S(1)}, s32[16]{0:T(128)}, u32[]{:S(2)}) copy-start(s32[16]{0:T(128)} %sym_ref.5) | copy-start | bytes 196
  46.7 37.1 %all-to-all-start.1 = ((f32[128,16,128]{2,1,0:T(8,128)}), f32[128,16,128]{2,1,0:T(8,128)S(1)}, u32[]{:S(2)}, u32[]{:S(2)}) async-start(f32[128,16,128]{2,1,0:T(8,128)} %bitcast.5), calls=%async_computation.1 | async-start | bytes 2097152 | tf_op jit(solution)/shard_map/all_to_all | solution.py:262
  84.0 8.3 %collective-permute-start = (f32[512,128]{1,0:T(8,128)S(1)}, f32[512,128]{1,0:T(8,128)S(1)}, u32[]{:S(2)}, u32[]{:S(2)}) collective-permute-start(f32[512,128]{1,0:T(8,128)S(1)} %get-tuple-element.10), channel_id=1, source_target_pairs={{0,1},{1,0},{2,3},{3,2},{4,5},{5,4},{6,7},{7,6},{8,9},{9,8},{10,11... | collective-permute-start | bytes 786440 | tf_op jit(solution)/shard_map/ppermute | solution.py:266
where the time goes:
time: 94.4 us; the launch traced here: 94.1 us
  blocking collectives  37.7 us (40%)
  waiting for transfers between devices  36.5 us (39%)
  Pallas kernels  10.3 us (11%)
  starting transfers between devices  5.85 us (6%)
  local copies, waits for them, and re-layouts  3.08 us (3%)
    all_to_all x1, blocking collectives, body(): series = lax.all_to_all(coef, 'ta', split_axis=0, concat_axis=0, tiled=True)  37.7 us
    all_to_all x1, waiting for transfers between devices, body(): lax.all_to_all(filtered, 'ta', split_axis=0, concat_axis=0, tiled=True)  31.7 us
    all_to_all x1, starting transfers between devices, body(): lax.all_to_all(filtered, 'ta', split_axis=0, concat_axis=0, tiled=True)  5.45 us
    ppermute x1, waiting for transfers between devices, body(): partner = lax.ppermute(other, 'lv', [(0, 1), (1, 0)])  4.8 us
    pallas_call x1, Pallas kernels, body(): call(time_kernel, [VMEM] * 8, shape(2048, 128), 3 * 4 * 512 * 256 * 256,...  4.06 us
    unnamed x24, local copies, waits for them, and re-layouts  3.08 us
    pallas_call x1, Pallas kernels, body(): call(waves_kernel, [SMEM, VMEM, VMEM], (shape(NLAT, BLOCK, NLON), shape(N...  3.07 us
  transfers between devices with their start and end apart: 2, of which 2 were waited for; matrix products, arithmetic and copies ran while one was open for 0% of the time, Pallas kernels for 3%

commit v1 on v0

--- a/solution.py
+++ b/solution.py
@@ -1,5 +1,3 @@
-import functools
-
 import jax
 import jax.numpy as jnp
 import ml_dtypes
@@ -17,8 +15,21 @@
 BLOCK = 32
 HALF = 16
 CENTRE = NPAIR - 1
+SHIFT = (2, 1, 4, 0)
 F32 = jnp.float32
 BF16 = jnp.bfloat16
+
+
+def member_order():
+    index = np.arange(128).reshape(4, 2, 8, 2)
+    return np.roll(index, SHIFT, axis=(0, 1, 2, 3)).reshape(-1)
+
+
+def exchange(blocks):
+    groups = [[int(member) for member in member_order()]]
+    return lax.all_to_all(
+        blocks, "ta", split_axis=0, concat_axis=0, axis_index_groups=groups, tiled=True
+    )
 
 
 def halves(table):
@@ -34,20 +45,20 @@
 
 
 def zonal_forward_table():
-    cosine, sine = turn(np.arange(KM), np.arange(NLON), NLON)
+    cosine, sine = turn(member_order(), np.arange(NLON), NLON)
     return halves(np.concatenate([cosine, -sine]) / NLON)
 
 
 def zonal_inverse_table():
-    cosine, sine = turn(np.arange(KM), np.arange(NLON), NLON)
-    doubled = np.where(np.arange(KM) == 0, 1.0, 2.0)[:, None]
+    cosine, sine = turn(member_order(), np.arange(NLON), NLON)
+    doubled = np.where(member_order() == 0, 1.0, 2.0)[:, None]
     return halves(np.concatenate([cosine * doubled, -sine * doubled]))
 
 
 def outer_tables():
-    cosine, sine = turn(np.arange(128), np.arange(128), 128)
+    cosine, sine = turn(np.arange(128), member_order(), 128)
     forward = np.block([[cosine, sine], [-sine, cosine]])
-    inverse = np.block([[cosine, -sine], [sine, cosine]]) / NT
+    inverse = np.block([[cosine.T, -sine.T], [sine.T, cosine.T]]) / NT
     return halves(forward), halves(inverse)
 
 
@@ -90,7 +101,19 @@
 COLS_COLS = ((0,), (0,))
 
 
-def zonal_kernel(sym_ref, wind_ref, table_ref, out_ref):
+def zonal_kernel(
+    sym_hbm, wind_hbm, table_hbm, out_ref, sym_ref, wind_ref, table_ref, arrived
+):
+    loads = [
+        pltpu.make_async_copy(source, target, arrived.at[i])
+        for i, (source, target) in enumerate(
+            ((sym_hbm, sym_ref), (wind_hbm, wind_ref), (table_hbm, table_ref))
+        )
+    ]
+    for load in loads:
+        load.start()
+    for load in loads:
+        load.wait()
     parts = []
     for j in range(NPAIR):
         sign = 1.0 - 2.0 * sym_ref[j].astype(F32)
@@ -218,6 +241,7 @@
 
 SMEM = pl.BlockSpec(memory_space=pltpu.SMEM)
 VMEM = pl.BlockSpec(memory_space=pltpu.VMEM)
+HBM = pl.BlockSpec(memory_space=pltpu.HBM)
 
 
 def call(kernel, in_specs, out_shapes, macs, moved, **kwargs):
@@ -231,6 +255,10 @@
     )
 
 
+def in_hbm(array):
+    return pltpu.with_memory_space_constraint(array, pltpu.HBM)
+
+
 def shape(*sizes):
     return jax.ShapeDtypeStruct(sizes, F32)
 
@@ -243,10 +271,21 @@
     spread = np.tile(np.eye(BLOCK), (1, 4)).astype(ml_dtypes.bfloat16)
     inverse_table = zonal_inverse_table()
 
-    coef = call(zonal_kernel, [SMEM, VMEM, VMEM], shape(1024, 128), 3 * 512 * 360 * 256, 3 << 20, out_specs=VMEM)(
-        sym_flag, record, zonal_forward_table()
-    )
-    series = lax.all_to_all(coef, "ta", split_axis=0, concat_axis=0, tiled=True)
+    coef = call(
+        zonal_kernel,
+        [HBM] * 3,
+        shape(1024, 128),
+        3 * 512 * 360 * 256,
+        3 << 20,
+        out_specs=VMEM,
+        scratch_shapes=[
+            pltpu.SMEM((NPAIR,), jnp.int32),
+            pltpu.VMEM((NLAT, BLOCK, NLON), F32),
+            pltpu.VMEM((2, 2 * KM, NLON), BF16),
+            pltpu.SemaphoreType.DMA((3,)),
+        ],
+    )(in_hbm(sym_flag), in_hbm(record), in_hbm(jnp.asarray(zonal_forward_table())))
+    series = exchange(coef)
     filtered = call(
         time_kernel, [VMEM] * 8, shape(2048, 128), 3 * 4 * 512 * 256 * 256, 4 << 20, out_specs=VMEM
     )(
@@ -259,7 +298,7 @@
         outer_i,
         twist_tables(),
     )
-    returned = lax.all_to_all(filtered, "ta", split_axis=0, concat_axis=0, tiled=True)
+    returned = exchange(filtered)
     own, other = call(
         pick_kernel, [SMEM, VMEM], (shape(512, 128), shape(512, 128)), 1 << 10, 1 << 20, out_specs=(VMEM, VMEM)
     )(level, returned)

time: 94.4 us -> 85.3 us (0.904)
  waiting for transfers between devices: 36.5 us -> 25.5 us
  starting transfers between devices: 5.85 us -> 16.2 us
  blocking collectives: 37.7 us -> 30.6 us
  local copies, waits for them, and re-layouts: 3.08 us -> 0.05 us
  Pallas kernels: 10.3 us -> 11.4 us
    all_to_all x1, starting transfers between devices: 5.45 us -> 15 us  [exchange(): lax.all_to_all(blocks, 'ta', split_axis=0, concat_axis=0, axis_index_grou...]
    all_to_all x1, waiting for transfers between devices: 31.7 us -> 22.8 us  [exchange(): lax.all_to_all(blocks, 'ta', split_axis=0, concat_axis=0, axis_index_grou...]
    all_to_all x1, blocking collectives: 37.7 us -> 30.6 us  [exchange(): lax.all_to_all(blocks, 'ta', split_axis=0, concat_axis=0, axis_index_grou...]
    unnamed x24 -> x18, local copies, waits for them, and re-layouts: 3.08 us -> 0.05 us
    ppermute x1, waiting for transfers between devices: 4.8 us -> 2.71 us  [body(): partner = lax.ppermute(other, 'lv', [(0, 1), (1, 0)])]
    pallas_call x1, Pallas kernels: 1.19 us -> 2.22 us  [body(): call(zonal_kernel, [HBM] * 3, shape(1024, 128), 3 * 512 * 360 * 256, 3 <<...]
  transfers between devices with their start and end apart: 2 -> 2, of which waited for: 2 -> 2; matrix products, arithmetic and copies ran while one was open for 0% -> 0% of each run, Pallas kernels for 3% -> 4%
where the time goes in v1:
time: 85.3 us; the launch traced here: 84.5 us
  blocking collectives  30.6 us (36%)
  waiting for transfers between devices  25.5 us (30%)
  starting transfers between devices  16.2 us (19%)
  Pallas kernels  11.4 us (13%)
    all_to_all x1, blocking collectives, exchange(): lax.all_to_all(blocks, 'ta', split_axis=0, concat_axis=0, axis_index_grou...  30.6 us
    all_to_all x1, waiting for transfers between devices, exchange(): lax.all_to_all(blocks, 'ta', split_axis=0, concat_axis=0, axis_index_grou...  22.8 us
    all_to_all x1, starting transfers between devices, exchange(): lax.all_to_all(blocks, 'ta', split_axis=0, concat_axis=0, axis_index_grou...  15 us
    pallas_call x1, Pallas kernels, body(): call(time_kernel, [VMEM] * 8, shape(2048, 128), 3 * 4 * 512 * 256 * 256,...  4.06 us
    pallas_call x1, Pallas kernels, body(): call(waves_kernel, [SMEM, VMEM, VMEM], (shape(NLAT, BLOCK, NLON), shape(N...  3.08 us
    ppermute x1, waiting for transfers between devices, body(): partner = lax.ppermute(other, 'lv', [(0, 1), (1, 0)])  2.71 us
    pallas_call x1, Pallas kernels, body(): call(zonal_kernel, [HBM] * 3, shape(1024, 128), 3 * 512 * 360 * 256, 3 <<...  2.22 us
    pallas_call x1, Pallas kernels, body(): call(shear_kernel, [SMEM, SMEM, VMEM, VMEM, VMEM], shape(NLAT, HALF, NLON...  1.83 us
  transfers between devices with their start and end apart: 2, of which 2 were waited for; matrix products, arithmetic and copies ran while one was open for 0% of the time, Pallas kernels for 4%

profile of v1, /device:TPU:1, one launch (start us, length us, event | category | flops | bytes accessed | tf_op | source)
XLA Modules:
  0.0 84.5 jit_solution(3349673867218523350)
XLA Ops:
  0.6 0.0 copy-start.2
  0.6 0.0 copy-start.3
  0.7 0.0 copy-start.4
  0.7 0.0 copy-start.5
  0.7 0.0 copy-start.6
  0.7 0.0 copy-start.7
  0.7 0.0 copy-start.8
  0.7 2.2 %shard_map.130 = f32[1024,128]{1,0:T(8,128)S(1)} custom-call(s32[16]{0:T(128)} %sym_ref.3, f32[31,32,360]{2,1,0:T(8,128)} %bitcast.21, bf16[2,256,360]{2,1,0:T(8,128)(2,1)} %constant.20.clone.table_hbm), custom_call_target="tpu_custom_call" | custom-call | flops 283115520 | bytes 3145728 | tf_op jit(solution)/shard_map/pallas_call | solution.py:274
  2.9 30.6 %all_to_all.22 = f32[128,8,128]{2,1,0:T(8,128)S(1)} all-to-all(f32[128,8,128]{2,1,0:T(8,128)S(1)} %bitcast.18), channel_id=1, replica_groups={{176,178,180,182,184,186,188,190,160,162,164,166,168,170,172,174,144,14..., dimensions={0} | all-to-all | bytes 1048576 | tf_op jit(solution)/shard_map/all_to_all | solution.py:30
  33.5 0.0 copy-done.2
  33.5 0.0 copy-done.3
  33.5 0.0 copy-done.4
  33.5 0.0 copy-done.5
  33.5 0.0 copy-done.6
  33.5 0.0 copy-done.7
  33.5 0.0 copy-done.8
  33.6 4.1 %shard_map.131 = f32[2048,128]{1,0:T(8,128)} custom-call(f32[1024,128]{1,0:T(8,128)S(1)} %bitcast.19, s32[2,32,128]{2,1,0:T(8,128)S(1)} %bitcast.20, bf16[32,128]{1,0:T(8,128)(2,1)S(1)} %copy-done.8, bf16[2,256,256]{2,1,0:T(8,128)(2,1)S(1)} %copy-done.3, bf16[2,256,256]{2,1,0:T(8,128)(2,1)S(1)} %copy-done.4, bf16[2,256,256]{2,1,0:T(8,128)(2,1)S(1)} %copy-done.5, ...), custom_call_target="tpu_custom_call" | custom-call | flops 805306368 | bytes 4194304 | tf_op jit(solution)/shard_map/pallas_call | solution.py:289
  37.6 0.0 copy-start
  37.6 0.0 copy-start.1
  37.6 15.0 %all-to-all-start.1 = ((f32[128,16,128]{2,1,0:T(8,128)}), f32[128,16,128]{2,1,0:T(8,128)S(1)}, u32[]{:S(2)}, u32[]{:S(2)}) async-start(f32[128,16,128]{2,1,0:T(8,128)} %bitcast.5), calls=%async_computation.1 | async-start | bytes 2097152 | tf_op jit(solution)/shard_map/all_to_all | solution.py:30
  52.6 22.8 %all-to-all-done.1 = f32[128,16,128]{2,1,0:T(8,128)S(1)} async-done(((f32[128,16,128]{2,1,0:T(8,128)}), f32[128,16,128]{2,1,0:T(8,128)S(1)}, u32[]{:S(2)}, u32[]{:S(2)}) %all-to-all-start.1) | async-done | bytes 1048608 | tf_op jit(solution)/shard_map/all_to_all | solution.py:30
  75.4 0.2 shard_map.133
  75.6 1.2 %collective-permute-start = (f32[512,128]{1,0:T(8,128)S(1)}, f32[512,128]{1,0:T(8,128)S(1)}, u32[]{:S(2)}, u32[]{:S(2)}) collective-permute-start(f32[512,128]{1,0:T(8,128)S(1)} %get-tuple-element.10), channel_id=1, source_target_pairs={{0,1},{1,0},{2,3},{3,2},{4,5},{5,4},{6,7},{7,6},{8,9},{9,8},{10,11... | collective-permute-start | bytes 786440 | tf_op jit(solution)/shard_map/ppermute | solution.py:305
  76.9 0.0 copy-done
  76.9 0.0 copy-done.1
  76.9 3.1 %shard_map.132 = (f32[31,32,360]{2,1,0:T(8,128)}, f32[31,32,360]{2,1,0:T(8,128)}) custom-call(s32[16]{0:T(128)S(1)} %copy-done.1, f32[2048,128]{1,0:T(8,128)S(1)} %bitcast.17, bf16[2,256,360]{2,1,0:T(8,128)(2,1)S(1)} %copy-done), custom_call_target="tpu_custom_call" | custom-call | flops 566231040 | bytes 5242880 | tf_op jit(solution)/shard_map/pallas_call | solution.py:307
  79.9 2.7 %collective-permute-done.partner_ref = f32[512,128]{1,0:T(8,128)S(1)} collective-permute-done((f32[512,128]{1,0:T(8,128)S(1)}, f32[512,128]{1,0:T(8,128)S(1)}, u32[]{:S(2)}, u32[]{:S(2)}) %collective-permute-start) | collective-permute-done | bytes 262176 | tf_op jit(solution)/shard_map/ppermute | solution.py:305
  82.7 1.8 %shard_map.134 = f32[31,16,360]{2,1,0:T(8,128)} custom-call(s32[1]{0:T(128)} %bitcast.11.level_ref, s32[16]{0:T(128)S(1)} %copy-done.1, f32[512,128]{1,0:T(8,128)S(1)} %get-tuple-element.9.own_ref, f32[512,128]{1,0:T(8,128)S(1)} %collective-permute-done.partner_ref, bf16[2,256,360]{2,1,0:T(8,128)(2,1)S(1)} %copy-done), custom_call_target="tpu_custom_call" | custom-call | flops 141557760 | bytes 2097152 | tf_op jit(solution)/shard_map/pallas_call | solution.py:316
Async XLA Ops:
  0.6 32.9 %copy-start.2 = (s32[2,1,4096]{2,1,0:T(1,128)S(1)}, s32[2,1,4096]{2,1,0:T(1,128)}, u32[]{:S(2)}) copy-start(s32[2,1,4096]{2,1,0:T(1,128)} %param.12) | copy-start | bytes 98308
  0.6 32.9 %copy-start.3 = (bf16[2,256,256]{2,1,0:T(8,128)(2,1)S(1)}, bf16[2,256,256]{2,1,0:T(8,128)(2,1)}, u32[]{:S(2)}) copy-start(bf16[2,256,256]{2,1,0:T(8,128)(2,1)} %constant.22.clone.outer_f) | copy-start | bytes 786436
  0.7 32.9 %copy-start.4 = (bf16[2,256,256]{2,1,0:T(8,128)(2,1)S(1)}, bf16[2,256,256]{2,1,0:T(8,128)(2,1)}, u32[]{:S(2)}) copy-start(bf16[2,256,256]{2,1,0:T(8,128)(2,1)} %constant.23.clone.inner_f) | copy-start | bytes 786436
  0.7 32.9 %copy-start.5 = (bf16[2,256,256]{2,1,0:T(8,128)(2,1)S(1)}, bf16[2,256,256]{2,1,0:T(8,128)(2,1)}, u32[]{:S(2)}) copy-start(bf16[2,256,256]{2,1,0:T(8,128)(2,1)} %constant.24.clone.inner_i) | copy-start | bytes 786436
  0.7 32.9 %copy-start.6 = (bf16[2,256,256]{2,1,0:T(8,128)(2,1)S(1)}, bf16[2,256,256]{2,1,0:T(8,128)(2,1)}, u32[]{:S(2)}) copy-start(bf16[2,256,256]{2,1,0:T(8,128)(2,1)} %constant.25.clone.outer_i) | copy-start | bytes 786436
  0.7 32.9 %copy-start.7 = (f32[4,128,128]{2,1,0:T(8,128)S(1)}, f32[4,128,128]{2,1,0:T(8,128)}, u32[]{:S(2)}) copy-start(f32[4,128,128]{2,1,0:T(8,128)} %constant.26.clone.twist_ref) | copy-start | bytes 786436
  0.7 32.8 %copy-start.8 = (bf16[32,128]{1,0:T(8,128)(2,1)S(1)}, bf16[32,128]{1,0:T(8,128)(2,1)}, u32[]{:S(2)}) copy-start(bf16[32,128]{1,0:T(8,128)(2,1)} %constant.21.clone.spread_ref) | copy-start | bytes 24580
  37.6 39.2 %copy-start = (bf16[2,256,360]{2,1,0:T(8,128)(2,1)S(1)}, bf16[2,256,360]{2,1,0:T(8,128)(2,1)}, u32[]{:S(2)}) copy-start(bf16[2,256,360]{2,1,0:T(8,128)(2,1)} %constant.27.clone.table_ref) | copy-start | bytes 1105924
  37.6 39.2 %copy-start.1 = (s32[16]{0:T(128)S(1)}, s32[16]{0:T(128)}, u32[]{:S(2)}) copy-start(s32[16]{0:T(128)} %sym_ref.3) | copy-start | bytes 196
  37.6 37.8 %all-to-all-start.1 = ((f32[128,16,128]{2,1,0:T(8,128)}), f32[128,16,128]{2,1,0:T(8,128)S(1)}, u32[]{:S(2)}, u32[]{:S(2)}) async-start(f32[128,16,128]{2,1,0:T(8,128)} %bitcast.5), calls=%async_computation.1 | async-start | bytes 2097152 | tf_op jit(solution)/shard_map/all_to_all | solution.py:30
  75.6 7.0 %collective-permute-start = (f32[512,128]{1,0:T(8,128)S(1)}, f32[512,128]{1,0:T(8,128)S(1)}, u32[]{:S(2)}, u32[]{:S(2)}) collective-permute-start(f32[512,128]{1,0:T(8,128)S(1)} %get-tuple-element.10), channel_id=1, source_target_pairs={{0,1},{1,0},{2,3},{3,2},{4,5},{5,4},{6,7},{7,6},{8,9},{9,8},{10,11... | collective-permute-start | bytes 786440 | tf_op jit(solution)/shard_map/ppermute | solution.py:305

commit v2 on v1

--- a/solution.py
+++ b/solution.py
@@ -102,7 +102,7 @@
 
 
 def zonal_kernel(
-    sym_hbm, wind_hbm, table_hbm, out_ref, sym_ref, wind_ref, table_ref, arrived
+    sym_hbm, wind_hbm, table_hbm, out_ref, sign_ref, sym_ref, wind_ref, table_ref, arrived
 ):
     loads = [
         pltpu.make_async_copy(source, target, arrived.at[i])
@@ -117,6 +117,7 @@
     parts = []
     for j in range(NPAIR):
         sign = 1.0 - 2.0 * sym_ref[j].astype(F32)
+        sign_ref[pl.ds(j, 1), :] = jnp.full((1, NLON), sign, F32)
         parts.append(0.5 * (wind_ref[CENTRE + j] + sign * wind_ref[CENTRE - j]))
     component = split(jnp.concatenate(parts, axis=0))
     coef = product((table_ref[0], table_ref[1]), component, ROWS_ROWS)
@@ -132,75 +133,85 @@
     def rows(ref):
         return ref[0], ref[1]
 
-    def wide(c):
-        return jnp.concatenate(
-            [series_ref[pl.ds(c * 4 + jq, 128, stride=8), :] for jq in range(4)], axis=1
-        )
-
-    operand = split(jnp.concatenate([wide(0), wide(1)], axis=0))
-    partial = product(rows(outer_f), operand, ROWS_COLS)
-    twisted = []
-    for jq in range(4):
-        lanes = slice(jq * 128, (jq + 1) * 128)
-        real, imag = partial[:128, lanes], partial[128:, lanes]
-        twisted.append(
-            jnp.concatenate(
+    def tile(value, c, q):
+        return value[c * 128 : (c + 1) * 128, q * 128 : (q + 1) * 128]
+
+    def square(tiles):
+        return jnp.concatenate([jnp.concatenate(row, axis=1) for row in tiles], axis=0)
+
+    def partial_dft(jh):
+        blocks = [
+            [series_ref[pl.ds(c * 4 + jh * 2 + q, 128, stride=8), :] for q in range(2)]
+            for c in range(2)
+        ]
+        return product(rows(outer_f), split(square(blocks)), ROWS_COLS)
+
+    def twist(value):
+        turned = []
+        for q in range(2):
+            real, imag = tile(value, 0, q), tile(value, 1, q)
+            turned.append(
                 [
                     real * twist_ref[0] - imag * twist_ref[1],
                     real * twist_ref[1] + imag * twist_ref[0],
-                ],
-                axis=1,
+                ]
             )
+        return square(turned)
+
+    low_lanes = lax.broadcasted_iota(jnp.int32, (128, 128), 1) < 64
+
+    def untwist(value):
+        turned = [[], []]
+        for q in range(2):
+            real, imag = tile(value, q, 0), tile(value, q, 1)
+            turned[0].append(real * twist_ref[2] - imag * twist_ref[3])
+            turned[1].append(real * twist_ref[3] + imag * twist_ref[2])
+        return square(
+            [
+                [
+                    jnp.where(low_lanes, first, pltpu.roll(second, 64, 1)),
+                    jnp.where(low_lanes, pltpu.roll(first, 64, 1), second),
+                ]
+                for first, second in turned
+            ]
         )
-    spectrum = product(split(jnp.concatenate(twisted, axis=0)), rows(inner_f), ROWS_COLS)
-    low_lanes = lax.broadcasted_iota(jnp.int32, (128, 128), 1) < 64
+
+    keeps = []
     for b in range(2):
         keep = lax.dot_general(
             mask_ref[b].astype(F32).astype(BF16),
             spread_ref[...],
             (COLS_COLS, ((), ())),
             preferred_element_type=F32,
-        )
-        keep = jnp.concatenate([jnp.concatenate([keep, keep], axis=1)] * 4, axis=0)
-        unwound = product(split(spectrum * keep), rows(inner_i), ROWS_COLS)
-        real_tiles, imag_tiles = [], []
-        for jq in range(4):
-            real = unwound[jq * 128 : (jq + 1) * 128, :128]
-            imag = unwound[jq * 128 : (jq + 1) * 128, 128:]
-            real_tiles.append(real * twist_ref[2] - imag * twist_ref[3])
-            imag_tiles.append(real * twist_ref[3] + imag * twist_ref[2])
-
-        def regroup(tiles):
-            first = [
-                jnp.where(low_lanes, tiles[2 * jh], pltpu.roll(tiles[2 * jh + 1], 64, 1))
-                for jh in range(2)
-            ]
-            second = [
-                jnp.where(low_lanes, pltpu.roll(tiles[2 * jh], 64, 1), tiles[2 * jh + 1])
-                for jh in range(2)
-            ]
-            return jnp.concatenate(first + second, axis=1)
-
-        stacked = jnp.concatenate([regroup(real_tiles), regroup(imag_tiles)], axis=0)
-        restored = product(rows(outer_i), split(stacked), ROWS_COLS)
+        ).astype(BF16)
+        keeps.append(square([[keep, keep], [keep, keep]]))
+
+    partial = [partial_dft(jh) for jh in range(2)]
+    twisted = [twist(value) for value in partial]
+    spectrum = [split(product(split(value), rows(inner_f), ROWS_COLS)) for value in twisted]
+    parts = [(b, jh) for b in range(2) for jh in range(2)]
+    unwound = [
+        product((spectrum[jh][0] * keeps[b], spectrum[jh][1] * keeps[b]), rows(inner_i), ROWS_COLS)
+        for b, jh in parts
+    ]
+    untwisted = [untwist(value) for value in unwound]
+    for (b, jh), value in zip(parts, untwisted):
+        restored = product(rows(outer_i), split(value), ROWS_COLS)
         for th in range(2):
             for c in range(2):
-                for jh in range(2):
-                    row = ((b * 2 + th) * 2 + c) * 2 + jh
-                    lanes = slice((th * 2 + jh) * 128, (th * 2 + jh + 1) * 128)
-                    out_ref[pl.ds(row, 128, stride=16), :] = restored[c * 128 : (c + 1) * 128, lanes]
-
-
-def write_rows(out_ref, waves, sym_ref):
+                row = ((b * 2 + th) * 2 + c) * 2 + jh
+                out_ref[pl.ds(row, 128, stride=16), :] = tile(restored, c, th)
+
+
+def write_rows(out_ref, waves, sign_ref):
     for j in range(NPAIR):
         block = waves[j * HALF : (j + 1) * HALF, :]
         out_ref[CENTRE + j] = block
         if j:
-            sign = 1.0 - 2.0 * sym_ref[j].astype(F32)
-            out_ref[CENTRE - j] = sign * block
-
-
-def waves_kernel(sym_ref, coef_ref, table_ref, kelvin_ref, mjo_ref):
+            out_ref[CENTRE - j] = sign_ref[pl.ds(j, 1), :] * block
+
+
+def waves_kernel(sign_ref, coef_ref, table_ref, kelvin_ref, mjo_ref):
     th = pl.program_id(0)
     table = (table_ref[0], table_ref[1])
     for b, out_ref in ((0, kelvin_ref), (1, mjo_ref)):
@@ -215,19 +226,19 @@
             ],
             axis=0,
         )
-        write_rows(out_ref, product(split(coef), table, COLS_COLS), sym_ref)
-
-
-def pick_kernel(level_ref, coef_ref, own_ref, other_ref):
-    level = level_ref[0]
+        write_rows(out_ref, product(split(coef), table, COLS_COLS), sign_ref)
+
+
+def pick_kernel(coef_ref, own_ref, other_ref):
+    level = lax.axis_index("lv")
     for out_ref, th in ((own_ref, level), (other_ref, 1 - level)):
         for r in range(4):
             out_ref[pl.ds(r * 128, 128), :] = coef_ref[pl.ds(8 + th * 4 + r, 128, stride=16), :]
 
 
-def shear_kernel(level_ref, sym_ref, own_ref, partner_ref, table_ref, out_ref):
-    sign = 2.0 * level_ref[0].astype(F32) - 1.0
-    apart = sign * (own_ref[...] - partner_ref[...])
+def shear_kernel(sign_ref, own_ref, partner_ref, table_ref, out_ref):
+    level_sign = jnp.where(lax.axis_index("lv") == 1, 1.0, -1.0)
+    apart = level_sign * (own_ref[...] - partner_ref[...])
     coef = jnp.concatenate(
         [
             jnp.concatenate([apart[c * 256 : c * 256 + 128], apart[c * 256 + 128 : c * 256 + 256]], axis=1)
@@ -236,10 +247,9 @@
         axis=0,
     )
     waves = product(split(coef), (table_ref[0], table_ref[1]), COLS_COLS)
-    write_rows(out_ref, waves, sym_ref)
-
-
-SMEM = pl.BlockSpec(memory_space=pltpu.SMEM)
+    write_rows(out_ref, waves, sign_ref)
+
+
 VMEM = pl.BlockSpec(memory_space=pltpu.VMEM)
 HBM = pl.BlockSpec(memory_space=pltpu.HBM)
 
@@ -264,20 +274,19 @@
 
 
 def body(wind_field, band_mask, sym_flag):
-    level = lax.axis_index("lv").astype(jnp.int32).reshape(1)
     record = jnp.transpose(wind_field[0], (1, 0, 2))
     outer_f, outer_i = outer_tables()
     inner_f, inner_i = inner_tables()
     spread = np.tile(np.eye(BLOCK), (1, 4)).astype(ml_dtypes.bfloat16)
     inverse_table = zonal_inverse_table()
 
-    coef = call(
+    coef, signs = call(
         zonal_kernel,
         [HBM] * 3,
-        shape(1024, 128),
+        (shape(1024, 128), shape(NPAIR, NLON)),
         3 * 512 * 360 * 256,
         3 << 20,
-        out_specs=VMEM,
+        out_specs=(VMEM, VMEM),
         scratch_shapes=[
             pltpu.SMEM((NPAIR,), jnp.int32),
             pltpu.VMEM((NLAT, BLOCK, NLON), F32),
@@ -300,22 +309,22 @@
     )
     returned = exchange(filtered)
     own, other = call(
-        pick_kernel, [SMEM, VMEM], (shape(512, 128), shape(512, 128)), 1 << 10, 1 << 20, out_specs=(VMEM, VMEM)
-    )(level, returned)
+        pick_kernel, [VMEM], (shape(512, 128), shape(512, 128)), 1 << 10, 1 << 20, out_specs=(VMEM, VMEM)
+    )(returned)
     partner = lax.ppermute(other, "lv", [(0, 1), (1, 0)])
     block = pl.BlockSpec((NLAT, HALF, NLON), lambda i: (0, i, 0))
     kelvin, mjo = call(
         waves_kernel,
-        [SMEM, VMEM, VMEM],
+        [VMEM, VMEM, VMEM],
         (shape(NLAT, BLOCK, NLON), shape(NLAT, BLOCK, NLON)),
         3 * 1024 * 360 * 256,
         5 << 20,
         grid=(2,),
         out_specs=(block, block),
-    )(sym_flag, returned, inverse_table)
+    )(signs, returned, inverse_table)
     shear = call(
-        shear_kernel, [SMEM, SMEM, VMEM, VMEM, VMEM], shape(NLAT, HALF, NLON), 3 * 256 * 360 * 256, 2 << 20, out_specs=VMEM
-    )(level, sym_flag, own, partner, inverse_table)
+        shear_kernel, [VMEM] * 4, shape(NLAT, HALF, NLON), 3 * 256 * 360 * 256, 2 << 20, out_specs=VMEM
+    )(signs, own, partner, inverse_table)
     return (
         jnp.transpose(kelvin, (1, 0, 2))[None],
         jnp.transpose(mjo, (1, 0, 2))[None],

time: 85.3 us -> 82.5 us (0.967)
  blocking collectives: 30.6 us -> 68.2 us
  waiting for transfers between devices: 25.5 us -> 3.31 us
  starting transfers between devices: 16.2 us -> 1.24 us
  Pallas kernels: 11.4 us -> 8.14 us
    all_to_all x1 -> x2, blocking collectives: 30.6 us -> 68.2 us  [exchange(): lax.all_to_all(blocks, 'ta', split_axis=0, concat_axis=0, axis_index_grou...]
    all_to_all x1 -> x0, waiting for transfers between devices: 22.8 us -> none  [exchange(): lax.all_to_all(blocks, 'ta', split_axis=0, concat_axis=0, axis_index_grou...]
    all_to_all x1 -> x0, starting transfers between devices: 15 us -> none  [exchange(): lax.all_to_all(blocks, 'ta', split_axis=0, concat_axis=0, axis_index_grou...]
    pallas_call x1, Pallas kernels: 4.06 us -> 1.97 us  [body(): call(time_kernel, [VMEM] * 8, shape(2048, 128), 3 * 4 * 512 * 256 * 256,...]
    pallas_call x4, Pallas kernels: 7.31 us -> 6.17 us  [the longest x1 2.49 us: body(): call(waves_kernel, [VMEM, VMEM, VMEM], (shape(NLAT, BLOCK, NLON), shape(N...]
  transfers between devices with their start and end apart: 2 -> 1, of which waited for: 2 -> 1; matrix products, arithmetic and copies ran while one was open for 0% -> 0% of each run, Pallas kernels for 4% -> 3%
where the time goes in v2:
time: 82.5 us; the launch traced here: 81.7 us
  blocking collectives  68.2 us (83%)
  Pallas kernels  8.14 us (10%)
  waiting for transfers between devices  3.31 us (4%)
  starting transfers between devices  1.24 us (2%)
    all_to_all x2, blocking collectives, exchange(): lax.all_to_all(blocks, 'ta', split_axis=0, concat_axis=0, axis_index_grou...  68.2 us
    ppermute x1, waiting for transfers between devices, body(): partner = lax.ppermute(other, 'lv', [(0, 1), (1, 0)])  3.31 us
    pallas_call x1, Pallas kernels, body(): call(waves_kernel, [VMEM, VMEM, VMEM], (shape(NLAT, BLOCK, NLON), shape(N...  2.49 us
    pallas_call x1, Pallas kernels, body(): call(zonal_kernel, [HBM] * 3, (shape(1024, 128), shape(NPAIR, NLON)), 3 *...  2.22 us
    pallas_call x1, Pallas kernels, body(): call(time_kernel, [VMEM] * 8, shape(2048, 128), 3 * 4 * 512 * 256 * 256,...  1.97 us
  transfers between devices with their start and end apart: 1, of which 1 were waited for; matrix products, arithmetic and copies ran while one was open for 0% of the time, Pallas kernels for 3%

profile of v2, /device:TPU:1, one launch (start us, length us, event | category | flops | bytes accessed | tf_op | source)
XLA Modules:
  0.0 81.7 jit_solution(7566658240056276452)
XLA Ops:
  0.6 0.0 copy-start.7
  0.6 0.0 copy-start.2
  0.7 0.0 copy-start.3
  0.7 0.0 copy-start.4
  0.7 0.0 copy-start.5
  0.7 0.0 copy-start.6
  0.7 0.0 copy-start.1
  0.7 2.2 %shard_map.130 = (f32[1024,128]{1,0:T(8,128)S(1)}, f32[16,360]{1,0:T(8,128)S(1)}) custom-call(s32[16]{0:T(128)} %sym_hbm.1, f32[31,32,360]{2,1,0:T(8,128)} %bitcast.21, bf16[2,256,360]{2,1,0:T(8,128)(2,1)} %constant.16.clone.table_hbm), custom_call_target="tpu_custom_call" | custom-call | flops 283115520 | bytes 3145728 | tf_op jit(solution)/shard_map/pallas_call | solution.py:283
  2.9 30.6 %all_to_all.22 = f32[128,8,128]{2,1,0:T(8,128)S(1)} all-to-all(f32[128,8,128]{2,1,0:T(8,128)S(1)} %bitcast.19), channel_id=1, replica_groups={{176,178,180,182,184,186,188,190,160,162,164,166,168,170,172,174,144,14..., dimensions={0} | all-to-all | bytes 1048576 | tf_op jit(solution)/shard_map/all_to_all | solution.py:30
  33.5 0.0 copy-done.7
  33.5 0.0 copy-done.2
  33.5 0.0 copy-done.3
  33.5 0.0 copy-done.4
  33.5 0.0 copy-done.5
  33.5 0.0 copy-done.6
  33.6 0.0 copy-done.1
  33.6 2.0 %shard_map.131 = f32[2048,128]{1,0:T(8,128)S(1)} custom-call(f32[1024,128]{1,0:T(8,128)S(1)} %bitcast.18, s32[2,32,128]{2,1,0:T(8,128)S(1)} %bitcast.20, bf16[32,128]{1,0:T(8,128)(2,1)S(1)} %copy-done.7, bf16[2,256,256]{2,1,0:T(8,128)(2,1)S(1)} %copy-done.2, bf16[2,256,256]{2,1,0:T(8,128)(2,1)S(1)} %copy-done.3, bf16[2,256,256]{2,1,0:T(8,128)(2,1)S(1)} %copy-done.4, ...), custom_call_target="tpu_custom_call" | custom-call | flops 805306368 | bytes 4194304 | tf_op jit(solution)/shard_map/pallas_call | solution.py:298
  35.5 0.0 copy-start
  35.6 37.6 %all_to_all.23 = f32[128,16,128]{2,1,0:T(8,128)S(1)} all-to-all(f32[128,16,128]{2,1,0:T(8,128)S(1)} %bitcast.17), channel_id=1, replica_groups={{176,178,180,182,184,186,188,190,160,162,164,166,168,170,172,174,144,14..., dimensions={0} | all-to-all | bytes 2097152 | tf_op jit(solution)/shard_map/all_to_all | solution.py:30
  73.2 0.2 shard_map.133
  73.3 1.2 %collective-permute-start = (f32[512,128]{1,0:T(8,128)S(1)}, f32[512,128]{1,0:T(8,128)S(1)}, u32[]{:S(2)}, u32[]{:S(2)}) collective-permute-start(f32[512,128]{1,0:T(8,128)S(1)} %get-tuple-element.14), channel_id=1, source_target_pairs={{0,1},{1,0},{2,3},{3,2},{4,5},{5,4},{6,7},{7,6},{8,9},{9,8},{10,11... | collective-permute-start | bytes 786440 | tf_op jit(solution)/shard_map/ppermute | solution.py:314
  74.6 0.0 copy-done
  74.6 2.5 %shard_map.132 = (f32[31,32,360]{2,1,0:T(8,128)}, f32[31,32,360]{2,1,0:T(8,128)}) custom-call(f32[16,360]{1,0:T(8,128)S(1)} %get-tuple-element.9.sign_ref, f32[2048,128]{1,0:T(8,128)S(1)} %bitcast.16, bf16[2,256,360]{2,1,0:T(8,128)(2,1)S(1)} %copy-done), custom_call_target="tpu_custom_call" | custom-call | flops 566231040 | bytes 5242880 | tf_op jit(solution)/shard_map/pallas_call | solution.py:316
  77.1 3.3 %collective-permute-done.partner_ref = f32[512,128]{1,0:T(8,128)S(1)} collective-permute-done((f32[512,128]{1,0:T(8,128)S(1)}, f32[512,128]{1,0:T(8,128)S(1)}, u32[]{:S(2)}, u32[]{:S(2)}) %collective-permute-start) | collective-permute-done | bytes 262176 | tf_op jit(solution)/shard_map/ppermute | solution.py:314
  80.4 1.3 %shard_map.134 = f32[31,16,360]{2,1,0:T(8,128)} custom-call(f32[16,360]{1,0:T(8,128)S(1)} %get-tuple-element.9.sign_ref, f32[512,128]{1,0:T(8,128)S(1)} %get-tuple-element.13.own_ref, f32[512,128]{1,0:T(8,128)S(1)} %collective-permute-done.partner_ref, bf16[2,256,360]{2,1,0:T(8,128)(2,1)S(1)} %copy-done), custom_call_target="tpu_custom_call" | custom-call | flops 141557760 | bytes 2097152 | tf_op jit(solution)/shard_map/pallas_call | solution.py:325
Async XLA Ops:
  0.6 32.9 %copy-start.7 = (bf16[32,128]{1,0:T(8,128)(2,1)S(1)}, bf16[32,128]{1,0:T(8,128)(2,1)}, u32[]{:S(2)}) copy-start(bf16[32,128]{1,0:T(8,128)(2,1)} %constant.17.clone.spread_ref) | copy-start | bytes 24580
  0.6 32.9 %copy-start.2 = (bf16[2,256,256]{2,1,0:T(8,128)(2,1)S(1)}, bf16[2,256,256]{2,1,0:T(8,128)(2,1)}, u32[]{:S(2)}) copy-start(bf16[2,256,256]{2,1,0:T(8,128)(2,1)} %constant.18.clone.outer_f) | copy-start | bytes 786436
  0.7 32.9 %copy-start.3 = (bf16[2,256,256]{2,1,0:T(8,128)(2,1)S(1)}, bf16[2,256,256]{2,1,0:T(8,128)(2,1)}, u32[]{:S(2)}) copy-start(bf16[2,256,256]{2,1,0:T(8,128)(2,1)} %constant.19.clone.inner_f) | copy-start | bytes 786436
  0.7 32.9 %copy-start.4 = (bf16[2,256,256]{2,1,0:T(8,128)(2,1)S(1)}, bf16[2,256,256]{2,1,0:T(8,128)(2,1)}, u32[]{:S(2)}) copy-start(bf16[2,256,256]{2,1,0:T(8,128)(2,1)} %constant.20.clone.inner_i) | copy-start | bytes 786436
  0.7 32.9 %copy-start.5 = (bf16[2,256,256]{2,1,0:T(8,128)(2,1)S(1)}, bf16[2,256,256]{2,1,0:T(8,128)(2,1)}, u32[]{:S(2)}) copy-start(bf16[2,256,256]{2,1,0:T(8,128)(2,1)} %constant.21.clone.outer_i) | copy-start | bytes 786436
  0.7 32.9 %copy-start.6 = (f32[4,128,128]{2,1,0:T(8,128)S(1)}, f32[4,128,128]{2,1,0:T(8,128)}, u32[]{:S(2)}) copy-start(f32[4,128,128]{2,1,0:T(8,128)} %constant.22.clone.twist_ref) | copy-start | bytes 786436
  0.7 32.9 %copy-start.1 = (s32[2,1,4096]{2,1,0:T(1,128)S(1)}, s32[2,1,4096]{2,1,0:T(1,128)}, u32[]{:S(2)}) copy-start(s32[2,1,4096]{2,1,0:T(1,128)} %param.12) | copy-start | bytes 98308
  35.5 39.0 %copy-start = (bf16[2,256,360]{2,1,0:T(8,128)(2,1)S(1)}, bf16[2,256,360]{2,1,0:T(8,128)(2,1)}, u32[]{:S(2)}) copy-start(bf16[2,256,360]{2,1,0:T(8,128)(2,1)} %constant.23.clone.table_ref) | copy-start | bytes 1105924
  73.3 7.0 %collective-permute-start = (f32[512,128]{1,0:T(8,128)S(1)}, f32[512,128]{1,0:T(8,128)S(1)}, u32[]{:S(2)}, u32[]{:S(2)}) collective-permute-start(f32[512,128]{1,0:T(8,128)S(1)} %get-tuple-element.14), channel_id=1, source_target_pairs={{0,1},{1,0},{2,3},{3,2},{4,5},{5,4},{6,7},{7,6},{8,9},{9,8},{10,11... | collective-permute-start | bytes 786440 | tf_op jit(solution)/shard_map/ppermute | solution.py:314

commit v3 on v2

--- a/solution.py
+++ b/solution.py
@@ -1,3 +1,5 @@
+import functools
+
 import jax
 import jax.numpy as jnp
 import ml_dtypes
@@ -15,18 +17,19 @@
 BLOCK = 32
 HALF = 16
 CENTRE = NPAIR - 1
-SHIFT = (2, 1, 4, 0)
+FIRST_TURN = (2, 1, 4, 0)
+SECOND_TURN = (2, 1, 4, 0)
 F32 = jnp.float32
 BF16 = jnp.bfloat16
 
 
-def member_order():
+def member_order(turn_by):
     index = np.arange(128).reshape(4, 2, 8, 2)
-    return np.roll(index, SHIFT, axis=(0, 1, 2, 3)).reshape(-1)
-
-
-def exchange(blocks):
-    groups = [[int(member) for member in member_order()]]
+    return np.roll(index, turn_by, axis=(0, 1, 2, 3)).reshape(-1)
+
+
+def exchange(blocks, turn_by):
+    groups = [[int(member) for member in member_order(turn_by)]]
     return lax.all_to_all(
         blocks, "ta", split_axis=0, concat_axis=0, axis_index_groups=groups, tiled=True
     )
@@ -45,20 +48,22 @@
 
 
 def zonal_forward_table():
-    cosine, sine = turn(member_order(), np.arange(NLON), NLON)
+    cosine, sine = turn(member_order(FIRST_TURN), np.arange(NLON), NLON)
     return halves(np.concatenate([cosine, -sine]) / NLON)
 
 
 def zonal_inverse_table():
-    cosine, sine = turn(member_order(), np.arange(NLON), NLON)
-    doubled = np.where(member_order() == 0, 1.0, 2.0)[:, None]
+    wavenumber = member_order(SECOND_TURN)
+    cosine, sine = turn(wavenumber, np.arange(NLON), NLON)
+    doubled = np.where(wavenumber == 0, 1.0, 2.0)[:, None]
     return halves(np.concatenate([cosine * doubled, -sine * doubled]))
 
 
 def outer_tables():
-    cosine, sine = turn(np.arange(128), member_order(), 128)
+    cosine, sine = turn(np.arange(128), member_order(FIRST_TURN), 128)
     forward = np.block([[cosine, sine], [-sine, cosine]])
-    inverse = np.block([[cosine.T, -sine.T], [sine.T, cosine.T]]) / NT
+    cosine, sine = turn(member_order(SECOND_TURN), np.arange(128), 128)
+    inverse = np.block([[cosine, -sine], [sine, cosine]]) / NT
     return halves(forward), halves(inverse)
 
 
@@ -229,25 +234,38 @@
         write_rows(out_ref, product(split(coef), table, COLS_COLS), sign_ref)
 
 
-def pick_kernel(coef_ref, own_ref, other_ref):
+def pick_kernel(coef_ref, *out_refs):
     level = lax.axis_index("lv")
-    for out_ref, th in ((own_ref, level), (other_ref, 1 - level)):
-        for r in range(4):
-            out_ref[pl.ds(r * 128, 128), :] = coef_ref[pl.ds(8 + th * 4 + r, 128, stride=16), :]
-
-
-def shear_kernel(sign_ref, own_ref, partner_ref, table_ref, out_ref):
+    for side, th in ((0, level), (1, 1 - level)):
+        for jh in range(2):
+            for c in range(2):
+                out_refs[side * 2 + jh][pl.ds(c * 128, 128), :] = coef_ref[
+                    pl.ds(8 + th * 4 + c * 2 + jh, 128, stride=16), :
+                ]
+
+
+def shear_kernel(jh, sign_ref, own_ref, partner_ref, table_ref, *rest):
+    out_hbm, rows_ref, sent = rest[-3:]
     level_sign = jnp.where(lax.axis_index("lv") == 1, 1.0, -1.0)
     apart = level_sign * (own_ref[...] - partner_ref[...])
-    coef = jnp.concatenate(
-        [
-            jnp.concatenate([apart[c * 256 : c * 256 + 128], apart[c * 256 + 128 : c * 256 + 256]], axis=1)
-            for c in range(2)
-        ],
-        axis=0,
-    )
-    waves = product(split(coef), (table_ref[0], table_ref[1]), COLS_COLS)
-    write_rows(out_ref, waves, sign_ref)
+    waves = product(split(apart), (table_ref[0], table_ref[1]), COLS_COLS)
+    centre = (7, 15)[jh]
+    for i in range(8):
+        j = jh * 8 + i
+        block = waves[i * HALF : (i + 1) * HALF, :]
+        rows_ref[7 + i + jh] = block
+        if j:
+            rows_ref[centre - j] = sign_ref[pl.ds(j, 1), :] * block
+    stores = [
+        pltpu.make_async_copy(
+            rows_ref.at[pl.ds(source, count)], out_hbm.at[pl.ds(target, count)], sent.at[i]
+        )
+        for i, (source, target, count) in enumerate((((0, 8, 15),), ((0, 0, 8), (8, 23, 8)))[jh])
+    ]
+    for store in stores:
+        store.start()
+    for store in stores:
+        store.wait()
 
 
 VMEM = pl.BlockSpec(memory_space=pltpu.VMEM)
@@ -294,7 +312,7 @@
             pltpu.SemaphoreType.DMA((3,)),
         ],
     )(in_hbm(sym_flag), in_hbm(record), in_hbm(jnp.asarray(zonal_forward_table())))
-    series = exchange(coef)
+    series = exchange(coef, FIRST_TURN)
     filtered = call(
         time_kernel, [VMEM] * 8, shape(2048, 128), 3 * 4 * 512 * 256 * 256, 4 << 20, out_specs=VMEM
     )(
@@ -307,11 +325,11 @@
         outer_i,
         twist_tables(),
     )
-    returned = exchange(filtered)
-    own, other = call(
-        pick_kernel, [VMEM], (shape(512, 128), shape(512, 128)), 1 << 10, 1 << 20, out_specs=(VMEM, VMEM)
+    returned = exchange(filtered, SECOND_TURN)
+    picked = call(
+        pick_kernel, [VMEM], (shape(256, 128),) * 4, 1 << 10, 1 << 20, out_specs=(VMEM,) * 4
     )(returned)
-    partner = lax.ppermute(other, "lv", [(0, 1), (1, 0)])
+    partner = [lax.ppermute(other, "lv", [(0, 1), (1, 0)]) for other in picked[2:]]
     block = pl.BlockSpec((NLAT, HALF, NLON), lambda i: (0, i, 0))
     kelvin, mjo = call(
         waves_kernel,
@@ -322,13 +340,27 @@
         grid=(2,),
         out_specs=(block, block),
     )(signs, returned, inverse_table)
-    shear = call(
-        shear_kernel, [VMEM] * 4, shape(NLAT, HALF, NLON), 3 * 256 * 360 * 256, 2 << 20, out_specs=VMEM
-    )(signs, own, partner, inverse_table)
+    shear = []
+    for jh in range(2):
+        shear = [
+            call(
+                functools.partial(shear_kernel, jh),
+                [VMEM] * 4 + [HBM] * jh,
+                shape(NLAT, HALF, NLON),
+                3 * 128 * 360 * 256,
+                1 << 20,
+                out_specs=HBM,
+                scratch_shapes=[
+                    pltpu.VMEM((16, HALF, NLON), F32),
+                    pltpu.SemaphoreType.DMA((2,)),
+                ],
+                input_output_aliases={4: 0} if jh else {},
+            )(signs, picked[jh], partner[jh], inverse_table, *shear)
+        ]
     return (
         jnp.transpose(kelvin, (1, 0, 2))[None],
         jnp.transpose(mjo, (1, 0, 2))[None],
-        jnp.transpose(shear, (1, 0, 2)),
+        jnp.transpose(shear[0], (1, 0, 2)),
     )
 
 

time: 82.5 us -> 82.2 us (level)
  waiting for transfers between devices: 3.31 us -> 1.92 us
  Pallas kernels: 8.14 us -> 9 us
    ppermute x1 -> x2, waiting for transfers between devices: 3.31 us -> 1.92 us  [body(): lax.ppermute(other, 'lv', [(0, 1), (1, 0)])]
    pallas_call x2 -> x3, Pallas kernels: 1.47 us -> 2.32 us  [the longest x2 2.14 us: body(): call(functools.partial(shear_kernel, jh), [VMEM] * 4 + [HBM] * jh, shape(...]
  transfers between devices with their start and end apart: 1 -> 2, of which waited for: 1 -> 2; matrix products, arithmetic and copies ran while one was open for 0% -> 0% of each run, Pallas kernels for 3% -> 4%
where the time goes in v3:
time: 82.2 us; the launch traced here: 81.4 us
  blocking collectives  68.2 us (83%)
  Pallas kernels  9 us (11%)
  waiting for transfers between devices  1.92 us (2%)
  starting transfers between devices  1.55 us (2%)
    all_to_all x2, blocking collectives, exchange(): lax.all_to_all(blocks, 'ta', split_axis=0, concat_axis=0, axis_index_grou...  68.2 us
    pallas_call x1, Pallas kernels, body(): call(waves_kernel, [VMEM, VMEM, VMEM], (shape(NLAT, BLOCK, NLON), shape(N...  2.49 us
    pallas_call x1, Pallas kernels, body(): call(zonal_kernel, [HBM] * 3, (shape(1024, 128), shape(NPAIR, NLON)), 3 *...  2.22 us
    pallas_call x2, Pallas kernels, body(): call(functools.partial(shear_kernel, jh), [VMEM] * 4 + [HBM] * jh, shape(...  2.14 us
    pallas_call x1, Pallas kernels, body(): call(time_kernel, [VMEM] * 8, shape(2048, 128), 3 * 4 * 512 * 256 * 256,...  1.97 us
    ppermute x2, waiting for transfers between devices, body(): lax.ppermute(other, 'lv', [(0, 1), (1, 0)])  1.92 us
  transfers between devices with their start and end apart: 2, of which 2 were waited for; matrix products, arithmetic and copies ran while one was open for 0% of the time, Pallas kernels for 4%

profile of v3, /device:TPU:1, one launch (start us, length us, event | category | flops | bytes accessed | tf_op | source)
XLA Modules:
  0.0 81.4 jit_solution(1821379897634914732)
XLA Ops:
  0.6 0.0 copy-start.7
  0.6 0.0 copy-start.2
  0.7 0.0 copy-start.3
  0.7 0.0 copy-start.4
  0.7 0.0 copy-start.5
  0.7 0.0 copy-start.6
  0.7 0.0 copy-start.1
  0.7 2.2 %shard_map.130 = (f32[1024,128]{1,0:T(8,128)S(1)}, f32[16,360]{1,0:T(8,128)S(1)}) custom-call(s32[16]{0:T(128)} %sym_hbm.1, f32[31,32,360]{2,1,0:T(8,128)} %bitcast.22, bf16[2,256,360]{2,1,0:T(8,128)(2,1)} %constant.16.clone.table_hbm), custom_call_target="tpu_custom_call" | custom-call | flops 283115520 | bytes 3145728 | tf_op jit(solution)/shard_map/pallas_call | solution.py:301
  2.9 30.6 %all_to_all.22 = f32[128,8,128]{2,1,0:T(8,128)S(1)} all-to-all(f32[128,8,128]{2,1,0:T(8,128)S(1)} %bitcast.19), channel_id=1, replica_groups={{176,178,180,182,184,186,188,190,160,162,164,166,168,170,172,174,144,14..., dimensions={0} | all-to-all | bytes 1048576 | tf_op jit(solution)/shard_map/all_to_all | solution.py:33
  33.5 0.0 copy-done.7
  33.5 0.0 copy-done.2
  33.5 0.0 copy-done.3
  33.5 0.0 copy-done.4
  33.5 0.0 copy-done.5
  33.5 0.0 copy-done.6
  33.6 0.0 copy-done.1
  33.6 2.0 %shard_map.131 = f32[2048,128]{1,0:T(8,128)S(1)} custom-call(f32[1024,128]{1,0:T(8,128)S(1)} %bitcast.18, s32[2,32,128]{2,1,0:T(8,128)S(1)} %bitcast.20, bf16[32,128]{1,0:T(8,128)(2,1)S(1)} %copy-done.7, bf16[2,256,256]{2,1,0:T(8,128)(2,1)S(1)} %copy-done.2, bf16[2,256,256]{2,1,0:T(8,128)(2,1)S(1)} %copy-done.3, bf16[2,256,256]{2,1,0:T(8,128)(2,1)S(1)} %copy-done.4, ...), custom_call_target="tpu_custom_call" | custom-call | flops 805306368 | bytes 4194304 | tf_op jit(solution)/shard_map/pallas_call | solution.py:316
  35.5 0.0 copy-start
  35.6 37.6 %all_to_all.23 = f32[128,16,128]{2,1,0:T(8,128)S(1)} all-to-all(f32[128,16,128]{2,1,0:T(8,128)S(1)} %bitcast.17), channel_id=1, replica_groups={{176,178,180,182,184,186,188,190,160,162,164,166,168,170,172,174,144,14..., dimensions={0} | all-to-all | bytes 2097152 | tf_op jit(solution)/shard_map/all_to_all | solution.py:33
  73.2 0.2 shard_map.133
  73.3 1.2 %collective-permute-start.1 = (f32[256,128]{1,0:T(8,128)S(1)}, f32[256,128]{1,0:T(8,128)S(1)}, u32[]{:S(2)}, u32[]{:S(2)}) collective-permute-start(f32[256,128]{1,0:T(8,128)S(1)} %get-tuple-element.18), channel_id=1, source_target_pairs={{0,1},{1,0},{2,3},{3,2},{4,5},{5,4},{6,7},{7,6},{8,9},{9,8},{10,11... | collective-permute-start | bytes 393224 | tf_op jit(solution)/shard_map/ppermute | solution.py:332
  74.6 0.3 collective-permute-start
  74.9 0.0 copy-done
  74.9 2.5 %shard_map.132 = (f32[31,32,360]{2,1,0:T(8,128)}, f32[31,32,360]{2,1,0:T(8,128)}) custom-call(f32[16,360]{1,0:T(8,128)S(1)} %get-tuple-element.11.sign_ref, f32[2048,128]{1,0:T(8,128)S(1)} %bitcast.16, bf16[2,256,360]{2,1,0:T(8,128)(2,1)S(1)} %copy-done), custom_call_target="tpu_custom_call" | custom-call | flops 566231040 | bytes 5242880 | tf_op jit(solution)/shard_map/pallas_call | solution.py:334
  77.4 0.2 collective-permute-done.1.partner_ref
  77.6 1.1 %shard_map.134.rest_0_ = f32[31,16,360]{2,1,0:T(8,128)} custom-call(f32[16,360]{1,0:T(8,128)S(1)} %get-tuple-element.11.sign_ref, f32[256,128]{1,0:T(8,128)S(1)} %get-tuple-element.17.own_ref, f32[256,128]{1,0:T(8,128)S(1)} %collective-permute-done.1.partner_ref, bf16[2,256,360]{2,1,0:T(8,128)(2,1)S(1)} %copy-done), custom_call_target="tpu_custom_call" | custom-call | flops 70778880 | bytes 1048576 | tf_op jit(solution)/shard_map/pallas_call | solution.py:346
  78.6 1.7 %collective-permute-done.partner_ref = f32[256,128]{1,0:T(8,128)S(1)} collective-permute-done((f32[256,128]{1,0:T(8,128)S(1)}, f32[256,128]{1,0:T(8,128)S(1)}, u32[]{:S(2)}, u32[]{:S(2)}) %collective-permute-start) | collective-permute-done | bytes 131104 | tf_op jit(solution)/shard_map/ppermute | solution.py:332
  80.4 1.1 %shard_map.135 = f32[31,16,360]{2,1,0:T(8,128)} custom-call(f32[16,360]{1,0:T(8,128)S(1)} %get-tuple-element.11.sign_ref, f32[256,128]{1,0:T(8,128)S(1)} %get-tuple-element.15.own_ref, f32[256,128]{1,0:T(8,128)S(1)} %collective-permute-done.partner_ref, bf16[2,256,360]{2,1,0:T(8,128)(2,1)S(1)} %copy-done, ...), custom_call_target="tpu_custom_call", output_to_operand_aliasing={{}: (4, {})} | custom-call | flops 70778880 | bytes 1048576 | tf_op jit(solution)/shard_map/pallas_call | solution.py:346
Async XLA Ops:
  0.6 32.9 %copy-start.7 = (bf16[32,128]{1,0:T(8,128)(2,1)S(1)}, bf16[32,128]{1,0:T(8,128)(2,1)}, u32[]{:S(2)}) copy-start(bf16[32,128]{1,0:T(8,128)(2,1)} %constant.17.clone.spread_ref) | copy-start | bytes 24580
  0.6 32.9 %copy-start.2 = (bf16[2,256,256]{2,1,0:T(8,128)(2,1)S(1)}, bf16[2,256,256]{2,1,0:T(8,128)(2,1)}, u32[]{:S(2)}) copy-start(bf16[2,256,256]{2,1,0:T(8,128)(2,1)} %constant.18.clone.outer_f) | copy-start | bytes 786436
  0.7 32.9 %copy-start.3 = (bf16[2,256,256]{2,1,0:T(8,128)(2,1)S(1)}, bf16[2,256,256]{2,1,0:T(8,128)(2,1)}, u32[]{:S(2)}) copy-start(bf16[2,256,256]{2,1,0:T(8,128)(2,1)} %constant.19.clone.inner_f) | copy-start | bytes 786436
  0.7 32.9 %copy-start.4 = (bf16[2,256,256]{2,1,0:T(8,128)(2,1)S(1)}, bf16[2,256,256]{2,1,0:T(8,128)(2,1)}, u32[]{:S(2)}) copy-start(bf16[2,256,256]{2,1,0:T(8,128)(2,1)} %constant.20.clone.inner_i) | copy-start | bytes 786436
  0.7 32.9 %copy-start.5 = (bf16[2,256,256]{2,1,0:T(8,128)(2,1)S(1)}, bf16[2,256,256]{2,1,0:T(8,128)(2,1)}, u32[]{:S(2)}) copy-start(bf16[2,256,256]{2,1,0:T(8,128)(2,1)} %constant.21.clone.outer_i) | copy-start | bytes 786436
  0.7 32.9 %copy-start.6 = (f32[4,128,128]{2,1,0:T(8,128)S(1)}, f32[4,128,128]{2,1,0:T(8,128)}, u32[]{:S(2)}) copy-start(f32[4,128,128]{2,1,0:T(8,128)} %constant.22.clone.twist_ref) | copy-start | bytes 786436
  0.7 32.9 %copy-start.1 = (s32[2,1,4096]{2,1,0:T(1,128)S(1)}, s32[2,1,4096]{2,1,0:T(1,128)}, u32[]{:S(2)}) copy-start(s32[2,1,4096]{2,1,0:T(1,128)} %param.12) | copy-start | bytes 98308
  35.5 39.3 %copy-start = (bf16[2,256,360]{2,1,0:T(8,128)(2,1)S(1)}, bf16[2,256,360]{2,1,0:T(8,128)(2,1)}, u32[]{:S(2)}) copy-start(bf16[2,256,360]{2,1,0:T(8,128)(2,1)} %constant.23.clone.table_ref) | copy-start | bytes 1105924
  73.3 4.2 %collective-permute-start.1 = (f32[256,128]{1,0:T(8,128)S(1)}, f32[256,128]{1,0:T(8,128)S(1)}, u32[]{:S(2)}, u32[]{:S(2)}) collective-permute-start(f32[256,128]{1,0:T(8,128)S(1)} %get-tuple-element.18), channel_id=1, source_target_pairs={{0,1},{1,0},{2,3},{3,2},{4,5},{5,4},{6,7},{7,6},{8,9},{9,8},{10,11... | collective-permute-start | bytes 393224 | tf_op jit(solution)/shard_map/ppermute | solution.py:332
  74.6 5.8 %collective-permute-start = (f32[256,128]{1,0:T(8,128)S(1)}, f32[256,128]{1,0:T(8,128)S(1)}, u32[]{:S(2)}, u32[]{:S(2)}) collective-permute-start(f32[256,128]{1,0:T(8,128)S(1)} %get-tuple-element.16), channel_id=1, source_target_pairs={{0,1},{1,0},{2,3},{3,2},{4,5},{5,4},{6,7},{7,6},{8,9},{9,8},{10,11... | collective-permute-start | bytes 393224 | tf_op jit(solution)/shard_map/ppermute | solution.py:332

commit v4 on v3

--- a/solution.py
+++ b/solution.py
@@ -17,8 +17,8 @@
 BLOCK = 32
 HALF = 16
 CENTRE = NPAIR - 1
-FIRST_TURN = (2, 1, 4, 0)
-SECOND_TURN = (2, 1, 4, 0)
+FIRST_TURN = (2, 1, 4, 1)
+SECOND_TURN = (2, 1, 4, 1)
 F32 = jnp.float32
 BF16 = jnp.bfloat16
 

time: 82.2 us -> 81.9 us (level)
  transfers between devices with their start and end apart: 2 -> 2, of which waited for: 2 -> 1; matrix products, arithmetic and copies ran while one was open for 0% -> 0% of each run, Pallas kernels for 4% -> 4%
where the time goes in v4:
time: 81.9 us; the launch traced here: 80.7 us
  blocking collectives  67.5 us (82%)
  Pallas kernels  9 us (11%)
  waiting for transfers between devices  1.87 us (2%)
  starting transfers between devices  1.55 us (2%)
    all_to_all x2, blocking collectives, exchange(): lax.all_to_all(blocks, 'ta', split_axis=0, concat_axis=0, axis_index_grou...  67.5 us
    pallas_call x1, Pallas kernels, body(): call(waves_kernel, [VMEM, VMEM, VMEM], (shape(NLAT, BLOCK, NLON), shape(N...  2.49 us
    pallas_call x1, Pallas kernels, body(): call(zonal_kernel, [HBM] * 3, (shape(1024, 128), shape(NPAIR, NLON)), 3 *...  2.22 us
    pallas_call x2, Pallas kernels, body(): call(functools.partial(shear_kernel, jh), [VMEM] * 4 + [HBM] * jh, shape(...  2.14 us
    pallas_call x1, Pallas kernels, body(): call(time_kernel, [VMEM] * 8, shape(2048, 128), 3 * 4 * 512 * 256 * 256,...  1.97 us
    ppermute x2, waiting for transfers between devices, body(): lax.ppermute(other, 'lv', [(0, 1), (1, 0)])  1.87 us
  transfers between devices with their start and end apart: 2, of which 1 were waited for; matrix products, arithmetic and copies ran while one was open for 0% of the time, Pallas kernels for 4%

profile of v4, /device:TPU:1, one launch (start us, length us, event | category | flops | bytes accessed | tf_op | source)
XLA Modules:
  0.0 80.7 jit_solution(8756476093417954757)
XLA Ops:
  0.6 0.0 copy-start.7
  0.6 0.0 copy-start.2
  0.7 0.0 copy-start.3
  0.7 0.0 copy-start.4
  0.7 0.0 copy-start.5
  0.7 0.0 copy-start.6
  0.7 0.0 copy-start.1
  0.7 2.2 %shard_map.130 = (f32[1024,128]{1,0:T(8,128)S(1)}, f32[16,360]{1,0:T(8,128)S(1)}) custom-call(s32[16]{0:T(128)} %sym_hbm.1, f32[31,32,360]{2,1,0:T(8,128)} %bitcast.22, bf16[2,256,360]{2,1,0:T(8,128)(2,1)} %constant.16.clone.table_hbm), custom_call_target="tpu_custom_call" | custom-call | flops 283115520 | bytes 3145728 | tf_op jit(solution)/shard_map/pallas_call | solution.py:301
  2.9 30.3 %all_to_all.22 = f32[128,8,128]{2,1,0:T(8,128)S(1)} all-to-all(f32[128,8,128]{2,1,0:T(8,128)S(1)} %bitcast.19), channel_id=1, replica_groups={{178,176,182,180,186,184,190,188,162,160,166,164,170,168,174,172,146,14..., dimensions={0} | all-to-all | bytes 1048576 | tf_op jit(solution)/shard_map/all_to_all | solution.py:33
  33.2 0.0 copy-done.7
  33.2 0.0 copy-done.2
  33.2 0.0 copy-done.3
  33.2 0.0 copy-done.4
  33.2 0.0 copy-done.5
  33.2 0.0 copy-done.6
  33.3 0.0 copy-done.1
  33.3 2.0 %shard_map.131 = f32[2048,128]{1,0:T(8,128)S(1)} custom-call(f32[1024,128]{1,0:T(8,128)S(1)} %bitcast.18, s32[2,32,128]{2,1,0:T(8,128)S(1)} %bitcast.20, bf16[32,128]{1,0:T(8,128)(2,1)S(1)} %copy-done.7, bf16[2,256,256]{2,1,0:T(8,128)(2,1)S(1)} %copy-done.2, bf16[2,256,256]{2,1,0:T(8,128)(2,1)S(1)} %copy-done.3, bf16[2,256,256]{2,1,0:T(8,128)(2,1)S(1)} %copy-done.4, ...), custom_call_target="tpu_custom_call" | custom-call | flops 805306368 | bytes 4194304 | tf_op jit(solution)/shard_map/pallas_call | solution.py:316
  35.3 0.0 copy-start
  35.3 37.2 %all_to_all.23 = f32[128,16,128]{2,1,0:T(8,128)S(1)} all-to-all(f32[128,16,128]{2,1,0:T(8,128)S(1)} %bitcast.17), channel_id=1, replica_groups={{178,176,182,180,186,184,190,188,162,160,166,164,170,168,174,172,146,14..., dimensions={0} | all-to-all | bytes 2097152 | tf_op jit(solution)/shard_map/all_to_all | solution.py:33
  72.5 0.2 shard_map.133
  72.7 1.2 %collective-permute-start.1 = (f32[256,128]{1,0:T(8,128)S(1)}, f32[256,128]{1,0:T(8,128)S(1)}, u32[]{:S(2)}, u32[]{:S(2)}) collective-permute-start(f32[256,128]{1,0:T(8,128)S(1)} %get-tuple-element.18), channel_id=1, source_target_pairs={{0,1},{1,0},{2,3},{3,2},{4,5},{5,4},{6,7},{7,6},{8,9},{9,8},{10,11... | collective-permute-start | bytes 393224 | tf_op jit(solution)/shard_map/ppermute | solution.py:332
  73.9 0.3 collective-permute-start
  74.2 0.0 copy-done
  74.2 2.5 %shard_map.132 = (f32[31,32,360]{2,1,0:T(8,128)}, f32[31,32,360]{2,1,0:T(8,128)}) custom-call(f32[16,360]{1,0:T(8,128)S(1)} %get-tuple-element.11.sign_ref, f32[2048,128]{1,0:T(8,128)S(1)} %bitcast.16, bf16[2,256,360]{2,1,0:T(8,128)(2,1)S(1)} %copy-done), custom_call_target="tpu_custom_call" | custom-call | flops 566231040 | bytes 5242880 | tf_op jit(solution)/shard_map/pallas_call | solution.py:334
  76.7 0.0 collective-permute-done.1.partner_ref
  76.7 1.1 %shard_map.134.rest_0_ = f32[31,16,360]{2,1,0:T(8,128)} custom-call(f32[16,360]{1,0:T(8,128)S(1)} %get-tuple-element.11.sign_ref, f32[256,128]{1,0:T(8,128)S(1)} %get-tuple-element.17.own_ref, f32[256,128]{1,0:T(8,128)S(1)} %collective-permute-done.1.partner_ref, bf16[2,256,360]{2,1,0:T(8,128)(2,1)S(1)} %copy-done), custom_call_target="tpu_custom_call" | custom-call | flops 70778880 | bytes 1048576 | tf_op jit(solution)/shard_map/pallas_call | solution.py:346
  77.8 1.9 %collective-permute-done.partner_ref = f32[256,128]{1,0:T(8,128)S(1)} collective-permute-done((f32[256,128]{1,0:T(8,128)S(1)}, f32[256,128]{1,0:T(8,128)S(1)}, u32[]{:S(2)}, u32[]{:S(2)}) %collective-permute-start) | collective-permute-done | bytes 131104 | tf_op jit(solution)/shard_map/ppermute | solution.py:332
  79.6 1.1 %shard_map.135 = f32[31,16,360]{2,1,0:T(8,128)} custom-call(f32[16,360]{1,0:T(8,128)S(1)} %get-tuple-element.11.sign_ref, f32[256,128]{1,0:T(8,128)S(1)} %get-tuple-element.15.own_ref, f32[256,128]{1,0:T(8,128)S(1)} %collective-permute-done.partner_ref, bf16[2,256,360]{2,1,0:T(8,128)(2,1)S(1)} %copy-done, ...), custom_call_target="tpu_custom_call", output_to_operand_aliasing={{}: (4, {})} | custom-call | flops 70778880 | bytes 1048576 | tf_op jit(solution)/shard_map/pallas_call | solution.py:346
Async XLA Ops:
  0.6 32.6 %copy-start.7 = (bf16[32,128]{1,0:T(8,128)(2,1)S(1)}, bf16[32,128]{1,0:T(8,128)(2,1)}, u32[]{:S(2)}) copy-start(bf16[32,128]{1,0:T(8,128)(2,1)} %constant.17.clone.spread_ref) | copy-start | bytes 24580
  0.6 32.6 %copy-start.2 = (bf16[2,256,256]{2,1,0:T(8,128)(2,1)S(1)}, bf16[2,256,256]{2,1,0:T(8,128)(2,1)}, u32[]{:S(2)}) copy-start(bf16[2,256,256]{2,1,0:T(8,128)(2,1)} %constant.18.clone.outer_f) | copy-start | bytes 786436
  0.7 32.6 %copy-start.3 = (bf16[2,256,256]{2,1,0:T(8,128)(2,1)S(1)}, bf16[2,256,256]{2,1,0:T(8,128)(2,1)}, u32[]{:S(2)}) copy-start(bf16[2,256,256]{2,1,0:T(8,128)(2,1)} %constant.19.clone.inner_f) | copy-start | bytes 786436
  0.7 32.6 %copy-start.4 = (bf16[2,256,256]{2,1,0:T(8,128)(2,1)S(1)}, bf16[2,256,256]{2,1,0:T(8,128)(2,1)}, u32[]{:S(2)}) copy-start(bf16[2,256,256]{2,1,0:T(8,128)(2,1)} %constant.20.clone.inner_i) | copy-start | bytes 786436
  0.7 32.6 %copy-start.5 = (bf16[2,256,256]{2,1,0:T(8,128)(2,1)S(1)}, bf16[2,256,256]{2,1,0:T(8,128)(2,1)}, u32[]{:S(2)}) copy-start(bf16[2,256,256]{2,1,0:T(8,128)(2,1)} %constant.21.clone.outer_i) | copy-start | bytes 786436
  0.7 32.6 %copy-start.6 = (f32[4,128,128]{2,1,0:T(8,128)S(1)}, f32[4,128,128]{2,1,0:T(8,128)}, u32[]{:S(2)}) copy-start(f32[4,128,128]{2,1,0:T(8,128)} %constant.22.clone.twist_ref) | copy-start | bytes 786436
  0.7 32.6 %copy-start.1 = (s32[2,1,4096]{2,1,0:T(1,128)S(1)}, s32[2,1,4096]{2,1,0:T(1,128)}, u32[]{:S(2)}) copy-start(s32[2,1,4096]{2,1,0:T(1,128)} %param.12) | copy-start | bytes 98308
  35.3 39.0 %copy-start = (bf16[2,256,360]{2,1,0:T(8,128)(2,1)S(1)}, bf16[2,256,360]{2,1,0:T(8,128)(2,1)}, u32[]{:S(2)}) copy-start(bf16[2,256,360]{2,1,0:T(8,128)(2,1)} %constant.23.clone.table_ref) | copy-start | bytes 1105924
  72.7 4.0 %collective-permute-start.1 = (f32[256,128]{1,0:T(8,128)S(1)}, f32[256,128]{1,0:T(8,128)S(1)}, u32[]{:S(2)}, u32[]{:S(2)}) collective-permute-start(f32[256,128]{1,0:T(8,128)S(1)} %get-tuple-element.18), channel_id=1, source_target_pairs={{0,1},{1,0},{2,3},{3,2},{4,5},{5,4},{6,7},{7,6},{8,9},{9,8},{10,11... | collective-permute-start | bytes 393224 | tf_op jit(solution)/shard_map/ppermute | solution.py:332
  73.9 5.8 %collective-permute-start = (f32[256,128]{1,0:T(8,128)S(1)}, f32[256,128]{1,0:T(8,128)S(1)}, u32[]{:S(2)}, u32[]{:S(2)}) collective-permute-start(f32[256,128]{1,0:T(8,128)S(1)} %get-tuple-element.16), channel_id=1, source_target_pairs={{0,1},{1,0},{2,3},{3,2},{4,5},{5,4},{6,7},{7,6},{8,9},{9,8},{10,11... | collective-permute-start | bytes 393224 | tf_op jit(solution)/shard_map/ppermute | solution.py:332

commit v5 on v4

--- a/solution.py
+++ b/solution.py
@@ -109,23 +109,38 @@
 def zonal_kernel(
     sym_hbm, wind_hbm, table_hbm, out_ref, sign_ref, sym_ref, wind_ref, table_ref, arrived
 ):
-    loads = [
-        pltpu.make_async_copy(source, target, arrived.at[i])
-        for i, (source, target) in enumerate(
-            ((sym_hbm, sym_ref), (wind_hbm, wind_ref), (table_hbm, table_ref))
+    cuts = (pl.ds(0, 256), pl.ds(256, NLON - 256))
+    flags = pltpu.make_async_copy(sym_hbm, sym_ref, arrived.at[0])
+    flags.start()
+    loads = []
+    for i, cut in enumerate(cuts):
+        pair = [
+            pltpu.make_async_copy(
+                source.at[:, :, cut], target.at[:, :, cut], arrived.at[1 + 2 * i + n]
+            )
+            for n, (source, target) in enumerate(((wind_hbm, wind_ref), (table_hbm, table_ref)))
+        ]
+        for load in pair:
+            load.start()
+        loads.append(pair)
+    flags.wait()
+    signs = [1.0 - 2.0 * sym_ref[j].astype(F32) for j in range(NPAIR)]
+    for j in range(NPAIR):
+        sign_ref[pl.ds(j, 1), :] = jnp.full((1, NLON), signs[j], F32)
+    terms = []
+    for cut, pair in zip(cuts, loads):
+        for load in pair:
+            load.wait()
+        component = jnp.concatenate(
+            [
+                0.5 * (wind_ref[CENTRE + j, :, cut] + signs[j] * wind_ref[CENTRE - j, :, cut])
+                for j in range(NPAIR)
+            ],
+            axis=0,
         )
-    ]
-    for load in loads:
-        load.start()
-    for load in loads:
-        load.wait()
-    parts = []
-    for j in range(NPAIR):
-        sign = 1.0 - 2.0 * sym_ref[j].astype(F32)
-        sign_ref[pl.ds(j, 1), :] = jnp.full((1, NLON), sign, F32)
-        parts.append(0.5 * (wind_ref[CENTRE + j] + sign * wind_ref[CENTRE - j]))
-    component = split(jnp.concatenate(parts, axis=0))
-    coef = product((table_ref[0], table_ref[1]), component, ROWS_ROWS)
+        table = (table_ref[0, :, cut], table_ref[1, :, cut])
+        terms.append(product(table, split(component), ROWS_ROWS))
+    coef = terms[0] + terms[1]
     for c in range(2):
         for jq in range(4):
             tile = coef[c * 128 : (c + 1) * 128, jq * 128 : (jq + 1) * 128]
@@ -235,19 +250,20 @@
 
 
 def pick_kernel(coef_ref, *out_refs):
+    first = 8 + (1 - lax.axis_index("lv")) * 4
+    for jh, out_ref in enumerate(out_refs):
+        for c in range(2):
+            out_ref[pl.ds(c * 128, 128), :] = coef_ref[pl.ds(first + c * 2 + jh, 128, stride=16), :]
+
+
+def shear_kernel(jh, sign_ref, coef_ref, partner_ref, table_ref, *rest):
+    out_hbm, rows_ref, sent = rest[-3:]
     level = lax.axis_index("lv")
-    for side, th in ((0, level), (1, 1 - level)):
-        for jh in range(2):
-            for c in range(2):
-                out_refs[side * 2 + jh][pl.ds(c * 128, 128), :] = coef_ref[
-                    pl.ds(8 + th * 4 + c * 2 + jh, 128, stride=16), :
-                ]
-
-
-def shear_kernel(jh, sign_ref, own_ref, partner_ref, table_ref, *rest):
-    out_hbm, rows_ref, sent = rest[-3:]
-    level_sign = jnp.where(lax.axis_index("lv") == 1, 1.0, -1.0)
-    apart = level_sign * (own_ref[...] - partner_ref[...])
+    level_sign = jnp.where(level == 1, 1.0, -1.0)
+    own = jnp.concatenate(
+        [coef_ref[pl.ds(8 + level * 4 + c * 2 + jh, 128, stride=16), :] for c in range(2)], axis=0
+    )
+    apart = level_sign * (own - partner_ref[...])
     waves = product(split(apart), (table_ref[0], table_ref[1]), COLS_COLS)
     centre = (7, 15)[jh]
     for i in range(8):
@@ -309,7 +325,7 @@
             pltpu.SMEM((NPAIR,), jnp.int32),
             pltpu.VMEM((NLAT, BLOCK, NLON), F32),
             pltpu.VMEM((2, 2 * KM, NLON), BF16),
-            pltpu.SemaphoreType.DMA((3,)),
+            pltpu.SemaphoreType.DMA((5,)),
         ],
     )(in_hbm(sym_flag), in_hbm(record), in_hbm(jnp.asarray(zonal_forward_table())))
     series = exchange(coef, FIRST_TURN)
@@ -327,9 +343,9 @@
     )
     returned = exchange(filtered, SECOND_TURN)
     picked = call(
-        pick_kernel, [VMEM], (shape(256, 128),) * 4, 1 << 10, 1 << 20, out_specs=(VMEM,) * 4
+        pick_kernel, [VMEM], (shape(256, 128),) * 2, 1 << 10, 1 << 20, out_specs=(VMEM,) * 2
     )(returned)
-    partner = [lax.ppermute(other, "lv", [(0, 1), (1, 0)]) for other in picked[2:]]
+    partner = [lax.ppermute(other, "lv", [(0, 1), (1, 0)]) for other in picked]
     block = pl.BlockSpec((NLAT, HALF, NLON), lambda i: (0, i, 0))
     kelvin, mjo = call(
         waves_kernel,
@@ -355,7 +371,7 @@
                     pltpu.SemaphoreType.DMA((2,)),
                 ],
                 input_output_aliases={4: 0} if jh else {},
-            )(signs, picked[jh], partner[jh], inverse_table, *shear)
+            )(signs, returned, partner[jh], inverse_table, *shear)
         ]
     return (
         jnp.transpose(kelvin, (1, 0, 2))[None],

time: 81.9 us -> 81.7 us (level)
  no operation moved by 1% of the time
where the time goes in v5:
time: 81.7 us; the launch traced here: 80.5 us
  blocking collectives  67.5 us (83%)
  Pallas kernels  8.83 us (11%)
  waiting for transfers between devices  1.85 us (2%)
  starting transfers between devices  1.55 us (2%)
    all_to_all x2, blocking collectives, exchange(): lax.all_to_all(blocks, 'ta', split_axis=0, concat_axis=0, axis_index_grou...  67.5 us
    pallas_call x1, Pallas kernels, body(): call(waves_kernel, [VMEM, VMEM, VMEM], (shape(NLAT, BLOCK, NLON), shape(N...  2.49 us
    pallas_call x2, Pallas kernels, body(): call(functools.partial(shear_kernel, jh), [VMEM] * 4 + [HBM] * jh, shape(...  2.18 us
    pallas_call x1, Pallas kernels, body(): call(zonal_kernel, [HBM] * 3, (shape(1024, 128), shape(NPAIR, NLON)), 3 *...  2.09 us
    pallas_call x1, Pallas kernels, body(): call(time_kernel, [VMEM] * 8, shape(2048, 128), 3 * 4 * 512 * 256 * 256,...  1.98 us
    ppermute x2, waiting for transfers between devices, body(): partner = [lax.ppermute(other, 'lv', [(0, 1), (1, 0)]) for other in picked]  1.85 us
  transfers between devices with their start and end apart: 2, of which 1 were waited for; matrix products, arithmetic and copies ran while one was open for 0% of the time, Pallas kernels for 4%

profile of v5, /device:TPU:1, one launch (start us, length us, event | category | flops | bytes accessed | tf_op | source)
XLA Modules:
  0.0 80.5 jit_solution(718670709578647252)
XLA Ops:
  0.6 0.0 copy-start.2
  0.6 0.0 copy-start.3
  0.7 0.0 copy-start.4
  0.7 0.0 copy-start.5
  0.7 0.0 copy-start.6
  0.7 0.0 copy-start.7
  0.7 0.0 copy-start.1
  0.7 2.1 %shard_map.130 = (f32[1024,128]{1,0:T(8,128)S(1)}, f32[16,360]{1,0:T(8,128)S(1)}) custom-call(s32[16]{0:T(128)} %sym_hbm.1, f32[31,32,360]{2,1,0:T(8,128)} %bitcast.24, bf16[2,256,360]{2,1,0:T(8,128)(2,1)} %constant.16.clone.table_hbm), custom_call_target="tpu_custom_call" | custom-call | flops 283115520 | bytes 3145728 | tf_op jit(solution)/shard_map/pallas_call | solution.py:317
  2.8 30.3 %all_to_all.22 = f32[128,8,128]{2,1,0:T(8,128)S(1)} all-to-all(f32[128,8,128]{2,1,0:T(8,128)S(1)} %bitcast.21), channel_id=1, replica_groups={{178,176,182,180,186,184,190,188,162,160,166,164,170,168,174,172,146,14..., dimensions={0} | all-to-all | bytes 1048576 | tf_op jit(solution)/shard_map/all_to_all | solution.py:33
  33.1 0.0 copy-done.2
  33.1 0.0 copy-done.3
  33.1 0.0 copy-done.4
  33.1 0.0 copy-done.5
  33.1 0.0 copy-done.6
  33.1 0.0 copy-done.7
  33.1 0.0 copy-done.1
  33.1 2.0 %shard_map.131 = f32[2048,128]{1,0:T(8,128)S(1)} custom-call(f32[1024,128]{1,0:T(8,128)S(1)} %bitcast.20, s32[2,32,128]{2,1,0:T(8,128)S(1)} %bitcast.22, bf16[32,128]{1,0:T(8,128)(2,1)S(1)} %copy-done.7, bf16[2,256,256]{2,1,0:T(8,128)(2,1)S(1)} %copy-done.6, bf16[2,256,256]{2,1,0:T(8,128)(2,1)S(1)} %copy-done.5, bf16[2,256,256]{2,1,0:T(8,128)(2,1)S(1)} %copy-done.4, ...), custom_call_target="tpu_custom_call" | custom-call | flops 805306368 | bytes 4194304 | tf_op jit(solution)/shard_map/pallas_call | solution.py:332
  35.1 0.0 copy-start
  35.1 37.2 %all_to_all.23 = f32[128,16,128]{2,1,0:T(8,128)S(1)} all-to-all(f32[128,16,128]{2,1,0:T(8,128)S(1)} %bitcast.19), channel_id=1, replica_groups={{178,176,182,180,186,184,190,188,162,160,166,164,170,168,174,172,146,14..., dimensions={0} | all-to-all | bytes 2097152 | tf_op jit(solution)/shard_map/all_to_all | solution.py:33
  72.3 0.1 shard_map.133
  72.4 1.2 %collective-permute-start.1 = (f32[256,128]{1,0:T(8,128)S(1)}, f32[256,128]{1,0:T(8,128)S(1)}, u32[]{:S(2)}, u32[]{:S(2)}) collective-permute-start(f32[256,128]{1,0:T(8,128)S(1)} %get-tuple-element.14), channel_id=1, source_target_pairs={{0,1},{1,0},{2,3},{3,2},{4,5},{5,4},{6,7},{7,6},{8,9},{9,8},{10,11... | collective-permute-start | bytes 393224 | tf_op jit(solution)/shard_map/ppermute | solution.py:348
  73.7 0.3 collective-permute-start
  74.0 0.0 copy-done
  74.0 2.5 %shard_map.132 = (f32[31,32,360]{2,1,0:T(8,128)}, f32[31,32,360]{2,1,0:T(8,128)}) custom-call(f32[16,360]{1,0:T(8,128)S(1)} %get-tuple-element.9.sign_ref, f32[2048,128]{1,0:T(8,128)S(1)} %bitcast.16, bf16[2,256,360]{2,1,0:T(8,128)(2,1)S(1)} %copy-done), custom_call_target="tpu_custom_call" | custom-call | flops 566231040 | bytes 5242880 | tf_op jit(solution)/shard_map/pallas_call | solution.py:350
  76.5 0.0 collective-permute-done.1.partner_ref
  76.5 1.1 %shard_map.134.rest_0_ = f32[31,16,360]{2,1,0:T(8,128)} custom-call(f32[16,360]{1,0:T(8,128)S(1)} %get-tuple-element.9.sign_ref, f32[2048,128]{1,0:T(8,128)S(1)} %bitcast.17, f32[256,128]{1,0:T(8,128)S(1)} %collective-permute-done.1.partner_ref, bf16[2,256,360]{2,1,0:T(8,128)(2,1)S(1)} %copy-done), custom_call_target="tpu_custom_call" | custom-call | flops 70778880 | bytes 1048576 | tf_op jit(solution)/shard_map/pallas_call | solution.py:362
  77.6 1.9 %collective-permute-done.partner_ref = f32[256,128]{1,0:T(8,128)S(1)} collective-permute-done((f32[256,128]{1,0:T(8,128)S(1)}, f32[256,128]{1,0:T(8,128)S(1)}, u32[]{:S(2)}, u32[]{:S(2)}) %collective-permute-start) | collective-permute-done | bytes 131104 | tf_op jit(solution)/shard_map/ppermute | solution.py:348
  79.4 1.1 %shard_map.135 = f32[31,16,360]{2,1,0:T(8,128)} custom-call(f32[16,360]{1,0:T(8,128)S(1)} %get-tuple-element.9.sign_ref, f32[2048,128]{1,0:T(8,128)S(1)} %bitcast.18, f32[256,128]{1,0:T(8,128)S(1)} %collective-permute-done.partner_ref, bf16[2,256,360]{2,1,0:T(8,128)(2,1)S(1)} %copy-done, ...), custom_call_target="tpu_custom_call", output_to_operand_aliasing={{}: (4, {})} | custom-call | flops 70778880 | bytes 1048576 | tf_op jit(solution)/shard_map/pallas_call | solution.py:362
Async XLA Ops:
  0.6 32.5 %copy-start.2 = (f32[4,128,128]{2,1,0:T(8,128)S(1)}, f32[4,128,128]{2,1,0:T(8,128)}, u32[]{:S(2)}) copy-start(f32[4,128,128]{2,1,0:T(8,128)} %constant.22.clone.twist_ref) | copy-start | bytes 786436
  0.6 32.5 %copy-start.3 = (bf16[2,256,256]{2,1,0:T(8,128)(2,1)S(1)}, bf16[2,256,256]{2,1,0:T(8,128)(2,1)}, u32[]{:S(2)}) copy-start(bf16[2,256,256]{2,1,0:T(8,128)(2,1)} %constant.21.clone.outer_i) | copy-start | bytes 786436
  0.7 32.4 %copy-start.4 = (bf16[2,256,256]{2,1,0:T(8,128)(2,1)S(1)}, bf16[2,256,256]{2,1,0:T(8,128)(2,1)}, u32[]{:S(2)}) copy-start(bf16[2,256,256]{2,1,0:T(8,128)(2,1)} %constant.20.clone.inner_i) | copy-start | bytes 786436
  0.7 32.4 %copy-start.5 = (bf16[2,256,256]{2,1,0:T(8,128)(2,1)S(1)}, bf16[2,256,256]{2,1,0:T(8,128)(2,1)}, u32[]{:S(2)}) copy-start(bf16[2,256,256]{2,1,0:T(8,128)(2,1)} %constant.19.clone.inner_f) | copy-start | bytes 786436
  0.7 32.4 %copy-start.6 = (bf16[2,256,256]{2,1,0:T(8,128)(2,1)S(1)}, bf16[2,256,256]{2,1,0:T(8,128)(2,1)}, u32[]{:S(2)}) copy-start(bf16[2,256,256]{2,1,0:T(8,128)(2,1)} %constant.18.clone.outer_f) | copy-start | bytes 786436
  0.7 32.4 %copy-start.7 = (bf16[32,128]{1,0:T(8,128)(2,1)S(1)}, bf16[32,128]{1,0:T(8,128)(2,1)}, u32[]{:S(2)}) copy-start(bf16[32,128]{1,0:T(8,128)(2,1)} %constant.17.clone.spread_ref) | copy-start | bytes 24580
  0.7 32.4 %copy-start.1 = (s32[2,1,4096]{2,1,0:T(1,128)S(1)}, s32[2,1,4096]{2,1,0:T(1,128)}, u32[]{:S(2)}) copy-start(s32[2,1,4096]{2,1,0:T(1,128)} %param.12) | copy-start | bytes 98308
  35.1 38.9 %copy-start = (bf16[2,256,360]{2,1,0:T(8,128)(2,1)S(1)}, bf16[2,256,360]{2,1,0:T(8,128)(2,1)}, u32[]{:S(2)}) copy-start(bf16[2,256,360]{2,1,0:T(8,128)(2,1)} %constant.23.clone.table_ref) | copy-start | bytes 1105924
  72.4 4.0 %collective-permute-start.1 = (f32[256,128]{1,0:T(8,128)S(1)}, f32[256,128]{1,0:T(8,128)S(1)}, u32[]{:S(2)}, u32[]{:S(2)}) collective-permute-start(f32[256,128]{1,0:T(8,128)S(1)} %get-tuple-element.14), channel_id=1, source_target_pairs={{0,1},{1,0},{2,3},{3,2},{4,5},{5,4},{6,7},{7,6},{8,9},{9,8},{10,11... | collective-permute-start | bytes 393224 | tf_op jit(solution)/shard_map/ppermute | solution.py:348
  73.7 5.8 %collective-permute-start = (f32[256,128]{1,0:T(8,128)S(1)}, f32[256,128]{1,0:T(8,128)S(1)}, u32[]{:S(2)}, u32[]{:S(2)}) collective-permute-start(f32[256,128]{1,0:T(8,128)S(1)} %get-tuple-element.13), channel_id=1, source_target_pairs={{0,1},{1,0},{2,3},{3,2},{4,5},{5,4},{6,7},{7,6},{8,9},{9,8},{10,11... | collective-permute-start | bytes 393224 | tf_op jit(solution)/shard_map/ppermute | solution.py:348

commit v6 on v5

--- a/solution.py
+++ b/solution.py
@@ -196,6 +196,8 @@
             ]
         )
 
+    partial = [partial_dft(jh) for jh in range(2)]
+    twisted = [twist(value) for value in partial]
     keeps = []
     for b in range(2):
         keep = lax.dot_general(
@@ -205,9 +207,6 @@
             preferred_element_type=F32,
         ).astype(BF16)
         keeps.append(square([[keep, keep], [keep, keep]]))
-
-    partial = [partial_dft(jh) for jh in range(2)]
-    twisted = [twist(value) for value in partial]
     spectrum = [split(product(split(value), rows(inner_f), ROWS_COLS)) for value in twisted]
     parts = [(b, jh) for b in range(2) for jh in range(2)]
     unwound = [
@@ -215,8 +214,8 @@
         for b, jh in parts
     ]
     untwisted = [untwist(value) for value in unwound]
-    for (b, jh), value in zip(parts, untwisted):
-        restored = product(rows(outer_i), split(value), ROWS_COLS)
+    final = [product(rows(outer_i), split(value), ROWS_COLS) for value in untwisted]
+    for (b, jh), restored in zip(parts, final):
         for th in range(2):
             for c in range(2):
                 row = ((b * 2 + th) * 2 + c) * 2 + jh
@@ -266,20 +265,28 @@
     apart = level_sign * (own - partner_ref[...])
     waves = product(split(apart), (table_ref[0], table_ref[1]), COLS_COLS)
     centre = (7, 15)[jh]
-    for i in range(8):
+    blocks = [waves[i * HALF : (i + 1) * HALF, :] for i in range(8)]
+    stores = []
+
+    def send(source, target, count):
+        stores.append(
+            pltpu.make_async_copy(
+                rows_ref.at[pl.ds(source, count)],
+                out_hbm.at[pl.ds(target, count)],
+                sent.at[len(stores)],
+            )
+        )
+        stores[-1].start()
+
+    for i, block in enumerate(blocks):
+        rows_ref[7 + i + jh] = block
+    if jh:
+        send(8, 23, 8)
+    for i, block in enumerate(blocks):
         j = jh * 8 + i
-        block = waves[i * HALF : (i + 1) * HALF, :]
-        rows_ref[7 + i + jh] = block
         if j:
             rows_ref[centre - j] = sign_ref[pl.ds(j, 1), :] * block
-    stores = [
-        pltpu.make_async_copy(
-            rows_ref.at[pl.ds(source, count)], out_hbm.at[pl.ds(target, count)], sent.at[i]
-        )
-        for i, (source, target, count) in enumerate((((0, 8, 15),), ((0, 0, 8), (8, 23, 8)))[jh])
-    ]
-    for store in stores:
-        store.start()
+    send(0, 8 * (1 - jh), 15 - 7 * jh)
     for store in stores:
         store.wait()
 

time: 81.7 us -> 81.6 us (level)
  no operation moved by 1% of the time
where the time goes in v6:
time: 81.6 us; the launch traced here: 80.5 us
  blocking collectives  67.5 us (83%)
  Pallas kernels  8.79 us (11%)
  waiting for transfers between devices  1.86 us (2%)
  starting transfers between devices  1.55 us (2%)
    all_to_all x2, blocking collectives, exchange(): lax.all_to_all(blocks, 'ta', split_axis=0, concat_axis=0, axis_index_grou...  67.5 us
    pallas_call x1, Pallas kernels, body(): call(waves_kernel, [VMEM, VMEM, VMEM], (shape(NLAT, BLOCK, NLON), shape(N...  2.48 us
    pallas_call x2, Pallas kernels, body(): call(functools.partial(shear_kernel, jh), [VMEM] * 4 + [HBM] * jh, shape(...  2.18 us
    pallas_call x1, Pallas kernels, body(): call(zonal_kernel, [HBM] * 3, (shape(1024, 128), shape(NPAIR, NLON)), 3 *...  2.09 us
    pallas_call x1, Pallas kernels, body(): call(time_kernel, [VMEM] * 8, shape(2048, 128), 3 * 4 * 512 * 256 * 256,...  1.94 us
    ppermute x2, waiting for transfers between devices, body(): partner = [lax.ppermute(other, 'lv', [(0, 1), (1, 0)]) for other in picked]  1.86 us
  transfers between devices with their start and end apart: 2, of which 1 were waited for; matrix products, arithmetic and copies ran while one was open for 0% of the time, Pallas kernels for 4%

profile of v6, /device:TPU:1, one launch (start us, length us, event | category | flops | bytes accessed | tf_op | source)
XLA Modules:
  0.0 80.5 jit_solution(4381056931264042046)
XLA Ops:
  0.6 0.0 copy-start.2
  0.6 0.0 copy-start.3
  0.7 0.0 copy-start.4
  0.7 0.0 copy-start.5
  0.7 0.0 copy-start.6
  0.7 0.0 copy-start.7
  0.7 0.0 copy-start.1
  0.7 2.1 %shard_map.130 = (f32[1024,128]{1,0:T(8,128)S(1)}, f32[16,360]{1,0:T(8,128)S(1)}) custom-call(s32[16]{0:T(128)} %sym_hbm.1, f32[31,32,360]{2,1,0:T(8,128)} %bitcast.24, bf16[2,256,360]{2,1,0:T(8,128)(2,1)} %constant.16.clone.table_hbm), custom_call_target="tpu_custom_call" | custom-call | flops 283115520 | bytes 3145728 | tf_op jit(solution)/shard_map/pallas_call | solution.py:324
  2.8 30.3 %all_to_all.22 = f32[128,8,128]{2,1,0:T(8,128)S(1)} all-to-all(f32[128,8,128]{2,1,0:T(8,128)S(1)} %bitcast.21), channel_id=1, replica_groups={{178,176,182,180,186,184,190,188,162,160,166,164,170,168,174,172,146,14..., dimensions={0} | all-to-all | bytes 1048576 | tf_op jit(solution)/shard_map/all_to_all | solution.py:33
  33.1 0.0 copy-done.2
  33.1 0.0 copy-done.3
  33.1 0.0 copy-done.4
  33.1 0.0 copy-done.5
  33.1 0.0 copy-done.6
  33.1 0.0 copy-done.7
  33.1 0.0 copy-done.1
  33.1 1.9 %shard_map.131 = f32[2048,128]{1,0:T(8,128)S(1)} custom-call(f32[1024,128]{1,0:T(8,128)S(1)} %bitcast.20, s32[2,32,128]{2,1,0:T(8,128)S(1)} %bitcast.22, bf16[32,128]{1,0:T(8,128)(2,1)S(1)} %copy-done.7, bf16[2,256,256]{2,1,0:T(8,128)(2,1)S(1)} %copy-done.6, bf16[2,256,256]{2,1,0:T(8,128)(2,1)S(1)} %copy-done.5, bf16[2,256,256]{2,1,0:T(8,128)(2,1)S(1)} %copy-done.4, ...), custom_call_target="tpu_custom_call" | custom-call | flops 805306368 | bytes 4194304 | tf_op jit(solution)/shard_map/pallas_call | solution.py:339
  35.1 0.0 copy-start
  35.1 37.2 %all_to_all.23 = f32[128,16,128]{2,1,0:T(8,128)S(1)} all-to-all(f32[128,16,128]{2,1,0:T(8,128)S(1)} %bitcast.19), channel_id=1, replica_groups={{178,176,182,180,186,184,190,188,162,160,166,164,170,168,174,172,146,14..., dimensions={0} | all-to-all | bytes 2097152 | tf_op jit(solution)/shard_map/all_to_all | solution.py:33
  72.3 0.1 shard_map.133
  72.4 1.2 %collective-permute-start.1 = (f32[256,128]{1,0:T(8,128)S(1)}, f32[256,128]{1,0:T(8,128)S(1)}, u32[]{:S(2)}, u32[]{:S(2)}) collective-permute-start(f32[256,128]{1,0:T(8,128)S(1)} %get-tuple-element.14), channel_id=1, source_target_pairs={{0,1},{1,0},{2,3},{3,2},{4,5},{5,4},{6,7},{7,6},{8,9},{9,8},{10,11... | collective-permute-start | bytes 393224 | tf_op jit(solution)/shard_map/ppermute | solution.py:355
  73.6 0.3 collective-permute-start
  74.0 0.0 copy-done
  74.0 2.5 %shard_map.132 = (f32[31,32,360]{2,1,0:T(8,128)}, f32[31,32,360]{2,1,0:T(8,128)}) custom-call(f32[16,360]{1,0:T(8,128)S(1)} %get-tuple-element.9.sign_ref, f32[2048,128]{1,0:T(8,128)S(1)} %bitcast.16, bf16[2,256,360]{2,1,0:T(8,128)(2,1)S(1)} %copy-done), custom_call_target="tpu_custom_call" | custom-call | flops 566231040 | bytes 5242880 | tf_op jit(solution)/shard_map/pallas_call | solution.py:357
  76.4 0.0 collective-permute-done.1.partner_ref
  76.4 1.1 %shard_map.134.rest_0_ = f32[31,16,360]{2,1,0:T(8,128)} custom-call(f32[16,360]{1,0:T(8,128)S(1)} %get-tuple-element.9.sign_ref, f32[2048,128]{1,0:T(8,128)S(1)} %bitcast.17, f32[256,128]{1,0:T(8,128)S(1)} %collective-permute-done.1.partner_ref, bf16[2,256,360]{2,1,0:T(8,128)(2,1)S(1)} %copy-done), custom_call_target="tpu_custom_call" | custom-call | flops 70778880 | bytes 1048576 | tf_op jit(solution)/shard_map/pallas_call | solution.py:369
  77.5 1.9 %collective-permute-done.partner_ref = f32[256,128]{1,0:T(8,128)S(1)} collective-permute-done((f32[256,128]{1,0:T(8,128)S(1)}, f32[256,128]{1,0:T(8,128)S(1)}, u32[]{:S(2)}, u32[]{:S(2)}) %collective-permute-start) | collective-permute-done | bytes 131104 | tf_op jit(solution)/shard_map/ppermute | solution.py:355
  79.4 1.1 %shard_map.135 = f32[31,16,360]{2,1,0:T(8,128)} custom-call(f32[16,360]{1,0:T(8,128)S(1)} %get-tuple-element.9.sign_ref, f32[2048,128]{1,0:T(8,128)S(1)} %bitcast.18, f32[256,128]{1,0:T(8,128)S(1)} %collective-permute-done.partner_ref, bf16[2,256,360]{2,1,0:T(8,128)(2,1)S(1)} %copy-done, ...), custom_call_target="tpu_custom_call", output_to_operand_aliasing={{}: (4, {})} | custom-call | flops 70778880 | bytes 1048576 | tf_op jit(solution)/shard_map/pallas_call | solution.py:369
Async XLA Ops:
  0.6 32.5 %copy-start.2 = (f32[4,128,128]{2,1,0:T(8,128)S(1)}, f32[4,128,128]{2,1,0:T(8,128)}, u32[]{:S(2)}) copy-start(f32[4,128,128]{2,1,0:T(8,128)} %constant.22.clone.twist_ref) | copy-start | bytes 786436
  0.6 32.5 %copy-start.3 = (bf16[2,256,256]{2,1,0:T(8,128)(2,1)S(1)}, bf16[2,256,256]{2,1,0:T(8,128)(2,1)}, u32[]{:S(2)}) copy-start(bf16[2,256,256]{2,1,0:T(8,128)(2,1)} %constant.21.clone.outer_i) | copy-start | bytes 786436
  0.7 32.4 %copy-start.4 = (bf16[2,256,256]{2,1,0:T(8,128)(2,1)S(1)}, bf16[2,256,256]{2,1,0:T(8,128)(2,1)}, u32[]{:S(2)}) copy-start(bf16[2,256,256]{2,1,0:T(8,128)(2,1)} %constant.20.clone.inner_i) | copy-start | bytes 786436
  0.7 32.4 %copy-start.5 = (bf16[2,256,256]{2,1,0:T(8,128)(2,1)S(1)}, bf16[2,256,256]{2,1,0:T(8,128)(2,1)}, u32[]{:S(2)}) copy-start(bf16[2,256,256]{2,1,0:T(8,128)(2,1)} %constant.19.clone.inner_f) | copy-start | bytes 786436
  0.7 32.4 %copy-start.6 = (bf16[2,256,256]{2,1,0:T(8,128)(2,1)S(1)}, bf16[2,256,256]{2,1,0:T(8,128)(2,1)}, u32[]{:S(2)}) copy-start(bf16[2,256,256]{2,1,0:T(8,128)(2,1)} %constant.18.clone.outer_f) | copy-start | bytes 786436
  0.7 32.4 %copy-start.7 = (bf16[32,128]{1,0:T(8,128)(2,1)S(1)}, bf16[32,128]{1,0:T(8,128)(2,1)}, u32[]{:S(2)}) copy-start(bf16[32,128]{1,0:T(8,128)(2,1)} %constant.17.clone.spread_ref) | copy-start | bytes 24580
  0.7 32.4 %copy-start.1 = (s32[2,1,4096]{2,1,0:T(1,128)S(1)}, s32[2,1,4096]{2,1,0:T(1,128)}, u32[]{:S(2)}) copy-start(s32[2,1,4096]{2,1,0:T(1,128)} %param.12) | copy-start | bytes 98308
  35.1 38.9 %copy-start = (bf16[2,256,360]{2,1,0:T(8,128)(2,1)S(1)}, bf16[2,256,360]{2,1,0:T(8,128)(2,1)}, u32[]{:S(2)}) copy-start(bf16[2,256,360]{2,1,0:T(8,128)(2,1)} %constant.23.clone.table_ref) | copy-start | bytes 1105924
  72.4 4.0 %collective-permute-start.1 = (f32[256,128]{1,0:T(8,128)S(1)}, f32[256,128]{1,0:T(8,128)S(1)}, u32[]{:S(2)}, u32[]{:S(2)}) collective-permute-start(f32[256,128]{1,0:T(8,128)S(1)} %get-tuple-element.14), channel_id=1, source_target_pairs={{0,1},{1,0},{2,3},{3,2},{4,5},{5,4},{6,7},{7,6},{8,9},{9,8},{10,11... | collective-permute-start | bytes 393224 | tf_op jit(solution)/shard_map/ppermute | solution.py:355
  73.6 5.8 %collective-permute-start = (f32[256,128]{1,0:T(8,128)S(1)}, f32[256,128]{1,0:T(8,128)S(1)}, u32[]{:S(2)}, u32[]{:S(2)}) collective-permute-start(f32[256,128]{1,0:T(8,128)S(1)} %get-tuple-element.13), channel_id=1, source_target_pairs={{0,1},{1,0},{2,3},{3,2},{4,5},{5,4},{6,7},{7,6},{8,9},{9,8},{10,11... | collective-permute-start | bytes 393224 | tf_op jit(solution)/shard_map/ppermute | solution.py:355

commit v7 on v6

--- a/solution.py
+++ b/solution.py
@@ -49,7 +49,7 @@
 
 def zonal_forward_table():
     cosine, sine = turn(member_order(FIRST_TURN), np.arange(NLON), NLON)
-    return halves(np.concatenate([cosine, -sine]) / NLON)
+    return halves(np.concatenate([cosine, -sine]) / NLON * 0.5)
 
 
 def zonal_inverse_table():
@@ -133,7 +133,7 @@
             load.wait()
         component = jnp.concatenate(
             [
-                0.5 * (wind_ref[CENTRE + j, :, cut] + signs[j] * wind_ref[CENTRE - j, :, cut])
+                wind_ref[CENTRE + j, :, cut] + signs[j] * wind_ref[CENTRE - j, :, cut]
                 for j in range(NPAIR)
             ],
             axis=0,

time: 81.6 us -> 81.6 us (level)
  no operation moved by 1% of the time
where the time goes in v7:
time: 81.6 us; the launch traced here: 80.5 us
  blocking collectives  67.5 us (83%)
  Pallas kernels  8.8 us (11%)
  waiting for transfers between devices  1.85 us (2%)
  starting transfers between devices  1.55 us (2%)
    all_to_all x2, blocking collectives, exchange(): lax.all_to_all(blocks, 'ta', split_axis=0, concat_axis=0, axis_index_grou...  67.5 us
    pallas_call x1, Pallas kernels, body(): call(waves_kernel, [VMEM, VMEM, VMEM], (shape(NLAT, BLOCK, NLON), shape(N...  2.49 us
    pallas_call x2, Pallas kernels, body(): call(functools.partial(shear_kernel, jh), [VMEM] * 4 + [HBM] * jh, shape(...  2.18 us
    pallas_call x1, Pallas kernels, body(): call(zonal_kernel, [HBM] * 3, (shape(1024, 128), shape(NPAIR, NLON)), 3 *...  2.09 us
    pallas_call x1, Pallas kernels, body(): call(time_kernel, [VMEM] * 8, shape(2048, 128), 3 * 4 * 512 * 256 * 256,...  1.94 us
    ppermute x2, waiting for transfers between devices, body(): partner = [lax.ppermute(other, 'lv', [(0, 1), (1, 0)]) for other in picked]  1.85 us
  transfers between devices with their start and end apart: 2, of which 1 were waited for; matrix products, arithmetic and copies ran while one was open for 0% of the time, Pallas kernels for 4%

profile of v7, /device:TPU:1, one launch (start us, length us, event | category | flops | bytes accessed | tf_op | source)
XLA Modules:
  0.0 80.5 jit_solution(1006412487526617947)
XLA Ops:
  0.6 0.0 copy-start.2
  0.6 0.0 copy-start.3
  0.7 0.0 copy-start.4
  0.7 0.0 copy-start.5
  0.7 0.0 copy-start.6
  0.7 0.0 copy-start.7
  0.7 0.0 copy-start.1
  0.7 2.1 %shard_map.130 = (f32[1024,128]{1,0:T(8,128)S(1)}, f32[16,360]{1,0:T(8,128)S(1)}) custom-call(s32[16]{0:T(128)} %sym_hbm.1, f32[31,32,360]{2,1,0:T(8,128)} %bitcast.24, bf16[2,256,360]{2,1,0:T(8,128)(2,1)} %constant.16.clone.table_hbm), custom_call_target="tpu_custom_call" | custom-call | flops 283115520 | bytes 3145728 | tf_op jit(solution)/shard_map/pallas_call | solution.py:324
  2.8 30.3 %all_to_all.22 = f32[128,8,128]{2,1,0:T(8,128)S(1)} all-to-all(f32[128,8,128]{2,1,0:T(8,128)S(1)} %bitcast.21), channel_id=1, replica_groups={{178,176,182,180,186,184,190,188,162,160,166,164,170,168,174,172,146,14..., dimensions={0} | all-to-all | bytes 1048576 | tf_op jit(solution)/shard_map/all_to_all | solution.py:33
  33.1 0.0 copy-done.2
  33.1 0.0 copy-done.3
  33.1 0.0 copy-done.4
  33.1 0.0 copy-done.5
  33.1 0.0 copy-done.6
  33.1 0.0 copy-done.7
  33.1 0.0 copy-done.1
  33.1 1.9 %shard_map.131 = f32[2048,128]{1,0:T(8,128)S(1)} custom-call(f32[1024,128]{1,0:T(8,128)S(1)} %bitcast.20, s32[2,32,128]{2,1,0:T(8,128)S(1)} %bitcast.22, bf16[32,128]{1,0:T(8,128)(2,1)S(1)} %copy-done.7, bf16[2,256,256]{2,1,0:T(8,128)(2,1)S(1)} %copy-done.6, bf16[2,256,256]{2,1,0:T(8,128)(2,1)S(1)} %copy-done.5, bf16[2,256,256]{2,1,0:T(8,128)(2,1)S(1)} %copy-done.4, ...), custom_call_target="tpu_custom_call" | custom-call | flops 805306368 | bytes 4194304 | tf_op jit(solution)/shard_map/pallas_call | solution.py:339
  35.1 0.0 copy-start
  35.1 37.2 %all_to_all.23 = f32[128,16,128]{2,1,0:T(8,128)S(1)} all-to-all(f32[128,16,128]{2,1,0:T(8,128)S(1)} %bitcast.19), channel_id=1, replica_groups={{178,176,182,180,186,184,190,188,162,160,166,164,170,168,174,172,146,14..., dimensions={0} | all-to-all | bytes 2097152 | tf_op jit(solution)/shard_map/all_to_all | solution.py:33
  72.3 0.1 shard_map.133
  72.4 1.2 %collective-permute-start.1 = (f32[256,128]{1,0:T(8,128)S(1)}, f32[256,128]{1,0:T(8,128)S(1)}, u32[]{:S(2)}, u32[]{:S(2)}) collective-permute-start(f32[256,128]{1,0:T(8,128)S(1)} %get-tuple-element.14), channel_id=1, source_target_pairs={{0,1},{1,0},{2,3},{3,2},{4,5},{5,4},{6,7},{7,6},{8,9},{9,8},{10,11... | collective-permute-start | bytes 393224 | tf_op jit(solution)/shard_map/ppermute | solution.py:355
  73.6 0.3 collective-permute-start
  74.0 0.0 copy-done
  74.0 2.5 %shard_map.132 = (f32[31,32,360]{2,1,0:T(8,128)}, f32[31,32,360]{2,1,0:T(8,128)}) custom-call(f32[16,360]{1,0:T(8,128)S(1)} %get-tuple-element.9.sign_ref, f32[2048,128]{1,0:T(8,128)S(1)} %bitcast.16, bf16[2,256,360]{2,1,0:T(8,128)(2,1)S(1)} %copy-done), custom_call_target="tpu_custom_call" | custom-call | flops 566231040 | bytes 5242880 | tf_op jit(solution)/shard_map/pallas_call | solution.py:357
  76.4 0.0 collective-permute-done.1.partner_ref
  76.5 1.1 %shard_map.134.rest_0_ = f32[31,16,360]{2,1,0:T(8,128)} custom-call(f32[16,360]{1,0:T(8,128)S(1)} %get-tuple-element.9.sign_ref, f32[2048,128]{1,0:T(8,128)S(1)} %bitcast.17, f32[256,128]{1,0:T(8,128)S(1)} %collective-permute-done.1.partner_ref, bf16[2,256,360]{2,1,0:T(8,128)(2,1)S(1)} %copy-done), custom_call_target="tpu_custom_call" | custom-call | flops 70778880 | bytes 1048576 | tf_op jit(solution)/shard_map/pallas_call | solution.py:369
  77.5 1.9 %collective-permute-done.partner_ref = f32[256,128]{1,0:T(8,128)S(1)} collective-permute-done((f32[256,128]{1,0:T(8,128)S(1)}, f32[256,128]{1,0:T(8,128)S(1)}, u32[]{:S(2)}, u32[]{:S(2)}) %collective-permute-start) | collective-permute-done | bytes 131104 | tf_op jit(solution)/shard_map/ppermute | solution.py:355
  79.4 1.1 %shard_map.135 = f32[31,16,360]{2,1,0:T(8,128)} custom-call(f32[16,360]{1,0:T(8,128)S(1)} %get-tuple-element.9.sign_ref, f32[2048,128]{1,0:T(8,128)S(1)} %bitcast.18, f32[256,128]{1,0:T(8,128)S(1)} %collective-permute-done.partner_ref, bf16[2,256,360]{2,1,0:T(8,128)(2,1)S(1)} %copy-done, ...), custom_call_target="tpu_custom_call", output_to_operand_aliasing={{}: (4, {})} | custom-call | flops 70778880 | bytes 1048576 | tf_op jit(solution)/shard_map/pallas_call | solution.py:369
Async XLA Ops:
  0.6 32.5 %copy-start.2 = (f32[4,128,128]{2,1,0:T(8,128)S(1)}, f32[4,128,128]{2,1,0:T(8,128)}, u32[]{:S(2)}) copy-start(f32[4,128,128]{2,1,0:T(8,128)} %constant.22.clone.twist_ref) | copy-start | bytes 786436
  0.6 32.5 %copy-start.3 = (bf16[2,256,256]{2,1,0:T(8,128)(2,1)S(1)}, bf16[2,256,256]{2,1,0:T(8,128)(2,1)}, u32[]{:S(2)}) copy-start(bf16[2,256,256]{2,1,0:T(8,128)(2,1)} %constant.21.clone.outer_i) | copy-start | bytes 786436
  0.7 32.4 %copy-start.4 = (bf16[2,256,256]{2,1,0:T(8,128)(2,1)S(1)}, bf16[2,256,256]{2,1,0:T(8,128)(2,1)}, u32[]{:S(2)}) copy-start(bf16[2,256,256]{2,1,0:T(8,128)(2,1)} %constant.20.clone.inner_i) | copy-start | bytes 786436
  0.7 32.4 %copy-start.5 = (bf16[2,256,256]{2,1,0:T(8,128)(2,1)S(1)}, bf16[2,256,256]{2,1,0:T(8,128)(2,1)}, u32[]{:S(2)}) copy-start(bf16[2,256,256]{2,1,0:T(8,128)(2,1)} %constant.19.clone.inner_f) | copy-start | bytes 786436
  0.7 32.4 %copy-start.6 = (bf16[2,256,256]{2,1,0:T(8,128)(2,1)S(1)}, bf16[2,256,256]{2,1,0:T(8,128)(2,1)}, u32[]{:S(2)}) copy-start(bf16[2,256,256]{2,1,0:T(8,128)(2,1)} %constant.18.clone.outer_f) | copy-start | bytes 786436
  0.7 32.4 %copy-start.7 = (bf16[32,128]{1,0:T(8,128)(2,1)S(1)}, bf16[32,128]{1,0:T(8,128)(2,1)}, u32[]{:S(2)}) copy-start(bf16[32,128]{1,0:T(8,128)(2,1)} %constant.17.clone.spread_ref) | copy-start | bytes 24580
  0.7 32.4 %copy-start.1 = (s32[2,1,4096]{2,1,0:T(1,128)S(1)}, s32[2,1,4096]{2,1,0:T(1,128)}, u32[]{:S(2)}) copy-start(s32[2,1,4096]{2,1,0:T(1,128)} %param.12) | copy-start | bytes 98308
  35.1 38.9 %copy-start = (bf16[2,256,360]{2,1,0:T(8,128)(2,1)S(1)}, bf16[2,256,360]{2,1,0:T(8,128)(2,1)}, u32[]{:S(2)}) copy-start(bf16[2,256,360]{2,1,0:T(8,128)(2,1)} %constant.23.clone.table_ref) | copy-start | bytes 1105924
  72.4 4.0 %collective-permute-start.1 = (f32[256,128]{1,0:T(8,128)S(1)}, f32[256,128]{1,0:T(8,128)S(1)}, u32[]{:S(2)}, u32[]{:S(2)}) collective-permute-start(f32[256,128]{1,0:T(8,128)S(1)} %get-tuple-element.14), channel_id=1, source_target_pairs={{0,1},{1,0},{2,3},{3,2},{4,5},{5,4},{6,7},{7,6},{8,9},{9,8},{10,11... | collective-permute-start | bytes 393224 | tf_op jit(solution)/shard_map/ppermute | solution.py:355
  73.6 5.8 %collective-permute-start = (f32[256,128]{1,0:T(8,128)S(1)}, f32[256,128]{1,0:T(8,128)S(1)}, u32[]{:S(2)}, u32[]{:S(2)}) collective-permute-start(f32[256,128]{1,0:T(8,128)S(1)} %get-tuple-element.13), channel_id=1, source_target_pairs={{0,1},{1,0},{2,3},{3,2},{4,5},{5,4},{6,7},{7,6},{8,9},{9,8},{10,11... | collective-permute-start | bytes 393224 | tf_op jit(solution)/shard_map/ppermute | solution.py:355

commit v8 on v7

--- a/solution.py
+++ b/solution.py
@@ -118,7 +118,7 @@
             pltpu.make_async_copy(
                 source.at[:, :, cut], target.at[:, :, cut], arrived.at[1 + 2 * i + n]
             )
-            for n, (source, target) in enumerate(((wind_hbm, wind_ref), (table_hbm, table_ref)))
+            for n, (source, target) in enumerate(((table_hbm, table_ref), (wind_hbm, wind_ref)))
         ]
         for load in pair:
             load.start()

time: 81.6 us -> 81.7 us (level)
  no operation moved by 1% of the time
where the time goes in v8:
time: 81.7 us; the launch traced here: 80.5 us
  blocking collectives  67.5 us (83%)
  Pallas kernels  8.83 us (11%)
  waiting for transfers between devices  1.85 us (2%)
  starting transfers between devices  1.55 us (2%)
    all_to_all x2, blocking collectives, exchange(): lax.all_to_all(blocks, 'ta', split_axis=0, concat_axis=0, axis_index_grou...  67.5 us
    pallas_call x1, Pallas kernels, body(): call(waves_kernel, [VMEM, VMEM, VMEM], (shape(NLAT, BLOCK, NLON), shape(N...  2.49 us
    pallas_call x2, Pallas kernels, body(): call(functools.partial(shear_kernel, jh), [VMEM] * 4 + [HBM] * jh, shape(...  2.18 us
    pallas_call x1, Pallas kernels, body(): call(zonal_kernel, [HBM] * 3, (shape(1024, 128), shape(NPAIR, NLON)), 3 *...  2.13 us
    pallas_call x1, Pallas kernels, body(): call(time_kernel, [VMEM] * 8, shape(2048, 128), 3 * 4 * 512 * 256 * 256,...  1.94 us
    ppermute x2, waiting for transfers between devices, body(): partner = [lax.ppermute(other, 'lv', [(0, 1), (1, 0)]) for other in picked]  1.85 us
  transfers between devices with their start and end apart: 2, of which 1 were waited for; matrix products, arithmetic and copies ran while one was open for 0% of the time, Pallas kernels for 4%

profile of v8, /device:TPU:1, one launch (start us, length us, event | category | flops | bytes accessed | tf_op | source)
XLA Modules:
  0.0 80.5 jit_solution(5131821058976341311)
XLA Ops:
  0.6 0.0 copy-start.2
  0.6 0.0 copy-start.3
  0.7 0.0 copy-start.4
  0.7 0.0 copy-start.5
  0.7 0.0 copy-start.6
  0.7 0.0 copy-start.7
  0.7 0.0 copy-start.1
  0.7 2.1 %shard_map.130 = (f32[1024,128]{1,0:T(8,128)S(1)}, f32[16,360]{1,0:T(8,128)S(1)}) custom-call(s32[16]{0:T(128)} %sym_hbm.1, f32[31,32,360]{2,1,0:T(8,128)} %bitcast.24, bf16[2,256,360]{2,1,0:T(8,128)(2,1)} %constant.16.clone.table_hbm), custom_call_target="tpu_custom_call" | custom-call | flops 283115520 | bytes 3145728 | tf_op jit(solution)/shard_map/pallas_call | solution.py:324
  2.9 30.3 %all_to_all.22 = f32[128,8,128]{2,1,0:T(8,128)S(1)} all-to-all(f32[128,8,128]{2,1,0:T(8,128)S(1)} %bitcast.21), channel_id=1, replica_groups={{178,176,182,180,186,184,190,188,162,160,166,164,170,168,174,172,146,14..., dimensions={0} | all-to-all | bytes 1048576 | tf_op jit(solution)/shard_map/all_to_all | solution.py:33
  33.1 0.0 copy-done.2
  33.1 0.0 copy-done.3
  33.1 0.0 copy-done.4
  33.1 0.0 copy-done.5
  33.1 0.0 copy-done.6
  33.2 0.0 copy-done.7
  33.2 0.0 copy-done.1
  33.2 1.9 %shard_map.131 = f32[2048,128]{1,0:T(8,128)S(1)} custom-call(f32[1024,128]{1,0:T(8,128)S(1)} %bitcast.20, s32[2,32,128]{2,1,0:T(8,128)S(1)} %bitcast.22, bf16[32,128]{1,0:T(8,128)(2,1)S(1)} %copy-done.7, bf16[2,256,256]{2,1,0:T(8,128)(2,1)S(1)} %copy-done.6, bf16[2,256,256]{2,1,0:T(8,128)(2,1)S(1)} %copy-done.5, bf16[2,256,256]{2,1,0:T(8,128)(2,1)S(1)} %copy-done.4, ...), custom_call_target="tpu_custom_call" | custom-call | flops 805306368 | bytes 4194304 | tf_op jit(solution)/shard_map/pallas_call | solution.py:339
  35.1 0.0 copy-start
  35.1 37.2 %all_to_all.23 = f32[128,16,128]{2,1,0:T(8,128)S(1)} all-to-all(f32[128,16,128]{2,1,0:T(8,128)S(1)} %bitcast.19), channel_id=1, replica_groups={{178,176,182,180,186,184,190,188,162,160,166,164,170,168,174,172,146,14..., dimensions={0} | all-to-all | bytes 2097152 | tf_op jit(solution)/shard_map/all_to_all | solution.py:33
  72.3 0.1 shard_map.133
  72.4 1.2 %collective-permute-start.1 = (f32[256,128]{1,0:T(8,128)S(1)}, f32[256,128]{1,0:T(8,128)S(1)}, u32[]{:S(2)}, u32[]{:S(2)}) collective-permute-start(f32[256,128]{1,0:T(8,128)S(1)} %get-tuple-element.14), channel_id=1, source_target_pairs={{0,1},{1,0},{2,3},{3,2},{4,5},{5,4},{6,7},{7,6},{8,9},{9,8},{10,11... | collective-permute-start | bytes 393224 | tf_op jit(solution)/shard_map/ppermute | solution.py:355
  73.7 0.3 collective-permute-start
  74.0 0.0 copy-done
  74.0 2.5 %shard_map.132 = (f32[31,32,360]{2,1,0:T(8,128)}, f32[31,32,360]{2,1,0:T(8,128)}) custom-call(f32[16,360]{1,0:T(8,128)S(1)} %get-tuple-element.9.sign_ref, f32[2048,128]{1,0:T(8,128)S(1)} %bitcast.16, bf16[2,256,360]{2,1,0:T(8,128)(2,1)S(1)} %copy-done), custom_call_target="tpu_custom_call" | custom-call | flops 566231040 | bytes 5242880 | tf_op jit(solution)/shard_map/pallas_call | solution.py:357
  76.5 0.0 collective-permute-done.1.partner_ref
  76.5 1.1 %shard_map.134.rest_0_ = f32[31,16,360]{2,1,0:T(8,128)} custom-call(f32[16,360]{1,0:T(8,128)S(1)} %get-tuple-element.9.sign_ref, f32[2048,128]{1,0:T(8,128)S(1)} %bitcast.17, f32[256,128]{1,0:T(8,128)S(1)} %collective-permute-done.1.partner_ref, bf16[2,256,360]{2,1,0:T(8,128)(2,1)S(1)} %copy-done), custom_call_target="tpu_custom_call" | custom-call | flops 70778880 | bytes 1048576 | tf_op jit(solution)/shard_map/pallas_call | solution.py:369
  77.6 1.9 %collective-permute-done.partner_ref = f32[256,128]{1,0:T(8,128)S(1)} collective-permute-done((f32[256,128]{1,0:T(8,128)S(1)}, f32[256,128]{1,0:T(8,128)S(1)}, u32[]{:S(2)}, u32[]{:S(2)}) %collective-permute-start) | collective-permute-done | bytes 131104 | tf_op jit(solution)/shard_map/ppermute | solution.py:355
  79.4 1.1 %shard_map.135 = f32[31,16,360]{2,1,0:T(8,128)} custom-call(f32[16,360]{1,0:T(8,128)S(1)} %get-tuple-element.9.sign_ref, f32[2048,128]{1,0:T(8,128)S(1)} %bitcast.18, f32[256,128]{1,0:T(8,128)S(1)} %collective-permute-done.partner_ref, bf16[2,256,360]{2,1,0:T(8,128)(2,1)S(1)} %copy-done, ...), custom_call_target="tpu_custom_call", output_to_operand_aliasing={{}: (4, {})} | custom-call | flops 70778880 | bytes 1048576 | tf_op jit(solution)/shard_map/pallas_call | solution.py:369
Async XLA Ops:
  0.6 32.5 %copy-start.2 = (f32[4,128,128]{2,1,0:T(8,128)S(1)}, f32[4,128,128]{2,1,0:T(8,128)}, u32[]{:S(2)}) copy-start(f32[4,128,128]{2,1,0:T(8,128)} %constant.22.clone.twist_ref) | copy-start | bytes 786436
  0.6 32.5 %copy-start.3 = (bf16[2,256,256]{2,1,0:T(8,128)(2,1)S(1)}, bf16[2,256,256]{2,1,0:T(8,128)(2,1)}, u32[]{:S(2)}) copy-start(bf16[2,256,256]{2,1,0:T(8,128)(2,1)} %constant.21.clone.outer_i) | copy-start | bytes 786436
  0.7 32.5 %copy-start.4 = (bf16[2,256,256]{2,1,0:T(8,128)(2,1)S(1)}, bf16[2,256,256]{2,1,0:T(8,128)(2,1)}, u32[]{:S(2)}) copy-start(bf16[2,256,256]{2,1,0:T(8,128)(2,1)} %constant.20.clone.inner_i) | copy-start | bytes 786436
  0.7 32.5 %copy-start.5 = (bf16[2,256,256]{2,1,0:T(8,128)(2,1)S(1)}, bf16[2,256,256]{2,1,0:T(8,128)(2,1)}, u32[]{:S(2)}) copy-start(bf16[2,256,256]{2,1,0:T(8,128)(2,1)} %constant.19.clone.inner_f) | copy-start | bytes 786436
  0.7 32.5 %copy-start.6 = (bf16[2,256,256]{2,1,0:T(8,128)(2,1)S(1)}, bf16[2,256,256]{2,1,0:T(8,128)(2,1)}, u32[]{:S(2)}) copy-start(bf16[2,256,256]{2,1,0:T(8,128)(2,1)} %constant.18.clone.outer_f) | copy-start | bytes 786436
  0.7 32.5 %copy-start.7 = (bf16[32,128]{1,0:T(8,128)(2,1)S(1)}, bf16[32,128]{1,0:T(8,128)(2,1)}, u32[]{:S(2)}) copy-start(bf16[32,128]{1,0:T(8,128)(2,1)} %constant.17.clone.spread_ref) | copy-start | bytes 24580
  0.7 32.5 %copy-start.1 = (s32[2,1,4096]{2,1,0:T(1,128)S(1)}, s32[2,1,4096]{2,1,0:T(1,128)}, u32[]{:S(2)}) copy-start(s32[2,1,4096]{2,1,0:T(1,128)} %param.12) | copy-start | bytes 98308
  35.1 38.9 %copy-start = (bf16[2,256,360]{2,1,0:T(8,128)(2,1)S(1)}, bf16[2,256,360]{2,1,0:T(8,128)(2,1)}, u32[]{:S(2)}) copy-start(bf16[2,256,360]{2,1,0:T(8,128)(2,1)} %constant.23.clone.table_ref) | copy-start | bytes 1105924
  72.4 4.0 %collective-permute-start.1 = (f32[256,128]{1,0:T(8,128)S(1)}, f32[256,128]{1,0:T(8,128)S(1)}, u32[]{:S(2)}, u32[]{:S(2)}) collective-permute-start(f32[256,128]{1,0:T(8,128)S(1)} %get-tuple-element.14), channel_id=1, source_target_pairs={{0,1},{1,0},{2,3},{3,2},{4,5},{5,4},{6,7},{7,6},{8,9},{9,8},{10,11... | collective-permute-start | bytes 393224 | tf_op jit(solution)/shard_map/ppermute | solution.py:355
  73.7 5.8 %collective-permute-start = (f32[256,128]{1,0:T(8,128)S(1)}, f32[256,128]{1,0:T(8,128)S(1)}, u32[]{:S(2)}, u32[]{:S(2)}) collective-permute-start(f32[256,128]{1,0:T(8,128)S(1)} %get-tuple-element.13), channel_id=1, source_target_pairs={{0,1},{1,0},{2,3},{3,2},{4,5},{5,4},{6,7},{7,6},{8,9},{9,8},{10,11... | collective-permute-start | bytes 393224 | tf_op jit(solution)/shard_map/ppermute | solution.py:355
